TPU v7x, 256 devices: a whole 4x4x8 slice. The times are simulated.
256 devices in a mesh: grp: 32 (over x, z), rep: 8 (over y, core).
Axes of the slice: x: 4, y: 4, z: 8, core: 2. Of those that a mesh axis runs over, the one named last changes fastest.
Arguments:
- frames: bfloat16 [8, 2048, 1280], P('rep', 'grp'), may hold values from -6 to 6
- destination: int32 [8, 2048, 1], P('rep', 'grp'), may hold values from 0 to 31; in each aligned block of 64 rows (0 to 63, 64 to 127, ..., all dimensions but the last counted through in order) at most 4 rows name the same one
- plan: int32 [8, 32], P('rep'), may hold values from 0 to 7, never falling along the last dimension, each value on 1 to 8 neighbouring positions
- norm_gain: float32 [1280], replicated, may hold values from 0.5 to 1.5
- w_qkv: bfloat16 [1280, 3072], P(None, 'rep'), as said below
- w_out: bfloat16 [1024, 1280], P('rep'), may hold values from -0.1875 to 0.1875
Outputs:
- attended: bfloat16 [8, 2048, 1280], P('rep', 'grp')
Inputs may be any that keep to these rules, and one draw needn't show every extreme that they name: `destination`: within the rows of one device no device is named more than 4 times, and in some draw blocks one is named exactly 4 times; every device of the replica is named by some row. `plan`: never falls along the devices; each group is 1 to 8 consecutive devices and one group has exactly 8. `w_qkv`: columns hold queries, keys and values in that order.
All inputs are finite; a program needn't handle non-finite values.
Results may differ from a plain program's by a relative error of at most 0.012.
The roundings to bfloat16 on the way count: a program that leaves them out, or rounds other values in their place, can miss the bound.
Values may be sent and summed in bfloat16 or wider, within the bound.
A program may use at most 64 MiB of HBM per device.

v0:
```python
import jax
import jax.numpy as jnp
from jax import lax
from jax.sharding import PartitionSpec as P

HEAD_DIM = 64


def shifted(shard, axis, by):
    count = lax.axis_size(axis)
    pairs = [(i, i + by) for i in range(count) if 0 <= i + by < count]
    return lax.ppermute(shard, axis, pairs)


def shards(frames, destination, plan, norm_gain, w_qkv, w_out):
    rows_in = frames[0]
    target = destination[0, :, 0]
    groups = plan[0]
    count = lax.axis_size("grp")
    me_index = lax.axis_index("grp")
    rows = rows_in.shape[0]
    width = rows_in.shape[1]
    cap = 2 * rows // count
    slots = count * cap
    reach = max(2, count // 4) - 1
    lanes = jnp.arange(count, dtype=jnp.int32)
    everyone = lax.all_gather(destination, "grp", axis=1, tiled=True)[0, :, 0]
    all_hot = (everyone[:, None] == lanes[None, :]).astype(jnp.int32).reshape(count, rows, count)
    counts = jnp.sum(all_hot, axis=1)
    live_table = (
        jnp.transpose(counts)[:, :, None] > jnp.arange(cap, dtype=jnp.int32)[None, None, :]
    ).reshape(count, slots)
    own_hot = (target[:, None] == lanes[None, :]).astype(jnp.int32)
    counted = jnp.cumsum(own_hot, axis=0)
    rank = jnp.sum((counted - 1) * own_hot, axis=1)
    position = target * cap + rank
    placing = (position[None, :] == jnp.arange(slots, dtype=jnp.int32)[:, None]).astype(
        jnp.bfloat16
    )
    outgoing = jnp.dot(placing, rows_in, preferred_element_type=jnp.float32).astype(jnp.bfloat16)
    arrived = lax.all_to_all(
        outgoing.reshape(count, cap, width), "grp", split_axis=0, concat_axis=0, tiled=True
    ).reshape(slots, width)
    values = arrived.astype(jnp.float32)
    mean = jnp.mean(values, axis=1, keepdims=True)
    centered = values - mean
    variance = jnp.mean(centered * centered, axis=1, keepdims=True)
    normed = (centered * lax.rsqrt(variance + 1e-05) * norm_gain[None, :]).astype(jnp.bfloat16)
    qkv = jnp.dot(
        normed, lax.all_gather(w_qkv, "rep", axis=1, tiled=True), preferred_element_type=jnp.float32
    ).astype(jnp.bfloat16)
    inner = qkv.shape[1] // 3
    heads = inner // HEAD_DIM
    query = qkv[:, :inner].reshape(slots, heads, HEAD_DIM)
    own_pair = qkv[:, inner:]
    mine = groups[me_index]

    def absorb(carry, pair, source):
        running, norm_sum, accum = carry
        inside = (source >= 0) & (source < count)
        clamped = jnp.clip(source, 0, count - 1)
        allowed = live_table[clamped] & (groups[clamped] == mine) & inside
        keys = pair[:, :inner].reshape(slots, heads, HEAD_DIM)
        vals = pair[:, inner:].reshape(slots, heads, HEAD_DIM)
        score = jnp.einsum(
            "shd,khd->hsk", query, keys, preferred_element_type=jnp.float32
        ) * HEAD_DIM ** (-0.5)
        score = jnp.where(allowed[None, None, :], score, -jnp.inf)
        updated = jnp.maximum(running, jnp.max(score, axis=2))
        factor = jnp.exp(running - updated)
        weights = jnp.exp(score - updated[:, :, None])
        norm_sum = norm_sum * factor + jnp.sum(weights, axis=2)
        mixed = jnp.einsum(
            "hsk,khd->hsd", weights.astype(jnp.bfloat16), vals, preferred_element_type=jnp.float32
        )
        accum = accum * factor[:, :, None] + mixed
        return (updated, norm_sum, accum)

    start_carry = (
        jnp.full((heads, slots), -jnp.inf, jnp.float32),
        jnp.zeros((heads, slots), jnp.float32),
        jnp.zeros((heads, slots, HEAD_DIM), jnp.float32),
    )
    carry = absorb(start_carry, own_pair, me_index)
    lower_pair = own_pair
    upper_pair = own_pair
    for hop in range(1, reach + 1):
        lower_pair = shifted(lower_pair, "grp", 1)
        carry = absorb(carry, lower_pair, me_index - hop)
        upper_pair = shifted(upper_pair, "grp", -1)
        carry = absorb(carry, upper_pair, me_index + hop)
    running, norm_sum, accum = carry
    context = accum / norm_sum[:, :, None]
    context = jnp.transpose(context, (1, 0, 2)).reshape(slots, inner).astype(jnp.bfloat16)
    projected = jnp.dot(
        context,
        lax.all_gather(w_out, "rep", axis=0, tiled=True),
        preferred_element_type=jnp.float32,
    ).astype(jnp.bfloat16)
    returned = lax.all_to_all(
        projected.reshape(count, cap, width), "grp", split_axis=0, concat_axis=0, tiled=True
    ).reshape(slots, width)
    picked = jnp.dot(jnp.transpose(placing), returned, preferred_element_type=jnp.float32).astype(
        jnp.bfloat16
    )
    return picked[None, :, :]


def solution(mesh):
    in_specs = (
        P("rep", "grp", None),
        P("rep", "grp", None),
        P("rep", None),
        P(),
        P(None, "rep"),
        P("rep", None),
    )
    out_specs = P("rep", "grp", None)
    return jax.shard_map(shards, mesh=mesh, in_specs=in_specs, out_specs=out_specs, check_vma=False)
```

profile of v0, /device:TPU:32, one launch (start us, length us, event | category | flops | bytes accessed | tf_op | source)
XLA Modules:
  0.0 270.4 jit_solution(1314701629380371866)
XLA Ops:
  12.7 11.2 %all-to-all-start = ((bf16[32,4,1280]{2,1,0:T(4,128)(2,1)}), bf16[32,4,1280]{2,1,0:T(4,128)(2,1)S(1)}, u32[]{:S(2)}, u32[]{:S(2)}) async-start(bf16[32,4,1280]{2,1,0:T(4,128)(2,1)} %reshape.973), calls=%async_computation | async-start | bytes 655360 | tf_op jit(solution)/shard_map/all_to_all | solution.py:41
  33.0 20.2 %all-reduce = s32[2048]{0:T(1024)S(1)} all-reduce(s32[2048]{0:T(1024)S(1)} %get-tuple-element.102), channel_id=1, replica_groups=mesh['grp'=32,'rep'=8] {'grp'}, use_global_device_ids=true, to_apply=%add | all-reduce | flops 2048 | bytes 16384
  67.1 4.5 %convolution_convert_fusion = bf16[128,3072]{1,0:T(8,128)(2,1)S(1)} fusion(bf16[1280,3072]{1,0:T(8,128)(2,1)} %all-gather.3.cloned.1.call-done, f32[128,1280]{1,0:T(8,128)S(1)} %reshape.1007, f32[1280]{0:T(1024)S(1)} %copy-done.25, f32[128]{0:T(128)S(1)} %rsqrt.12, f32[128]{0:T(128)S(1)} %div.18), kind=kOutput, calls=%fused_computation | convolution fusion | flops 1007681536 | bytes 9312256 | tf_op jit(solution)/shard_map/dot_general | solution.py:49
  72.5 3.4 %collective-permute-start.1 = (bf16[128,2048]{1,0:T(8,128)(2,1)}, bf16[128,2048]{1,0:T(8,128)(2,1)}, u32[]{:S(2)}, u32[]{:S(2)}) collective-permute-start(bf16[128,2048]{1,0:T(8,128)(2,1)} %slice.133), channel_id=1, source_target_pairs={{8,0},{16,8},{24,16},{32,24},{40,32},{48,40},{56,48},{64,56},{72,6... | collective-permute-start | bytes 1572872 | tf_op jit(solution)/shard_map/ppermute | solution.py:12
  76.0 2.7 %collective-permute-start = (bf16[128,2048]{1,0:T(8,128)(2,1)}, bf16[128,2048]{1,0:T(8,128)(2,1)}, u32[]{:S(2)}, u32[]{:S(2)}) collective-permute-start(bf16[128,2048]{1,0:T(8,128)(2,1)} %slice.133), channel_id=1, source_target_pairs={{0,8},{8,16},{16,24},{24,32},{32,40},{40,48},{48,56},{56,64},{64,7... | collective-permute-start | bytes 1572872 | tf_op jit(solution)/shard_map/ppermute | solution.py:12
  79.8 5.2 %collective-permute-done.1 = bf16[128,2048]{1,0:T(8,128)(2,1)} collective-permute-done((bf16[128,2048]{1,0:T(8,128)(2,1)}, bf16[128,2048]{1,0:T(8,128)(2,1)}, u32[]{:S(2)}, u32[]{:S(2)}) %collective-permute-start.1) | collective-permute-done | bytes 524320 | tf_op jit(solution)/shard_map/ppermute | solution.py:12
  86.3 2.8 %collective-permute-start.3 = (bf16[128,2048]{1,0:T(8,128)(2,1)}, bf16[128,2048]{1,0:T(8,128)(2,1)}, u32[]{:S(2)}, u32[]{:S(2)}) collective-permute-start(bf16[128,2048]{1,0:T(8,128)(2,1)} %collective-permute-done.1), channel_id=1, source_target_pairs={{8,0},{16,8},{24,16},{32,24},{40,32},{48,40},{56,48},{64,56},{72,6... | collective-permute-start | bytes 1572872 | tf_op jit(solution)/shard_map/ppermute | solution.py:12
  89.4 3.1 %collective-permute-start.2 = (bf16[128,2048]{1,0:T(8,128)(2,1)}, bf16[128,2048]{1,0:T(8,128)(2,1)}, u32[]{:S(2)}, u32[]{:S(2)}) collective-permute-start(bf16[128,2048]{1,0:T(8,128)(2,1)} %collective-permute-done), channel_id=1, source_target_pairs={{0,8},{8,16},{16,24},{24,32},{32,40},{40,48},{48,56},{56,64},{64,7... | collective-permute-start | bytes 1572872 | tf_op jit(solution)/shard_map/ppermute | solution.py:12
  97.1 2.3 fusion.164
  99.4 1.9 fusion.144
  102.4 1.9 fusion.141
  106.0 3.6 %collective-permute-start.5 = (bf16[128,2048]{1,0:T(8,128)(2,1)}, bf16[128,2048]{1,0:T(8,128)(2,1)}, u32[]{:S(2)}, u32[]{:S(2)}) collective-permute-start(bf16[128,2048]{1,0:T(8,128)(2,1)} %collective-permute-done.3), channel_id=1, source_target_pairs={{8,0},{16,8},{24,16},{32,24},{40,32},{48,40},{56,48},{64,56},{72,6... | collective-permute-start | bytes 1572872 | tf_op jit(solution)/shard_map/ppermute | solution.py:12
  109.6 2.3 collective-permute-start.4
  113.3 2.3 fusion.161
  116.7 1.8 copy.170
  118.5 1.9 fusion.145
  122.2 4.4 %collective-permute-start.7 = (bf16[128,2048]{1,0:T(8,128)(2,1)}, bf16[128,2048]{1,0:T(8,128)(2,1)}, u32[]{:S(2)}, u32[]{:S(2)}) collective-permute-start(bf16[128,2048]{1,0:T(8,128)(2,1)} %collective-permute-done.5), channel_id=1, source_target_pairs={{8,0},{16,8},{24,16},{32,24},{40,32},{48,40},{56,48},{64,56},{72,6... | collective-permute-start | bytes 1572872 | tf_op jit(solution)/shard_map/ppermute | solution.py:12
  126.5 2.3 fusion.158
  128.8 2.1 collective-permute-start.6
  131.0 1.9 fusion.140
  138.2 2.3 fusion.159
  140.5 1.9 fusion.146
  142.3 1.8 copy.184
  144.1 1.9 fusion.139
  146.0 1.8 copy.181
  147.8 4.5 %collective-permute-start.9 = (bf16[128,2048]{1,0:T(8,128)(2,1)}, bf16[128,2048]{1,0:T(8,128)(2,1)}, u32[]{:S(2)}, u32[]{:S(2)}) collective-permute-start(bf16[128,2048]{1,0:T(8,128)(2,1)} %collective-permute-done.7), channel_id=1, source_target_pairs={{8,0},{16,8},{24,16},{32,24},{40,32},{48,40},{56,48},{64,56},{72,6... | collective-permute-start | bytes 1572872 | tf_op jit(solution)/shard_map/ppermute | solution.py:12
  152.3 2.5 collective-permute-start.8
  154.9 2.3 fusion.156
  157.2 2.3 fusion.157
  163.1 1.9 fusion.147
  166.8 4.3 %collective-permute-start.11 = (bf16[128,2048]{1,0:T(8,128)(2,1)}, bf16[128,2048]{1,0:T(8,128)(2,1)}, u32[]{:S(2)}, u32[]{:S(2)}) collective-permute-start(bf16[128,2048]{1,0:T(8,128)(2,1)} %collective-permute-done.9), channel_id=1, source_target_pairs={{8,0},{16,8},{24,16},{32,24},{40,32},{48,40},{56,48},{64,56},{72,6... | collective-permute-start | bytes 1572872 | tf_op jit(solution)/shard_map/ppermute | solution.py:12
  171.1 2.3 fusion.154
  173.4 1.9 fusion.138
  177.0 2.9 %collective-permute-start.10 = (bf16[128,2048]{1,0:T(8,128)(2,1)}, bf16[128,2048]{1,0:T(8,128)(2,1)}, u32[]{:S(2)}, u32[]{:S(2)}) collective-permute-start(bf16[128,2048]{1,0:T(8,128)(2,1)} %collective-permute-done.8), channel_id=1, source_target_pairs={{0,8},{8,16},{16,24},{24,32},{32,40},{40,48},{48,56},{56,64},{64,7... | collective-permute-start | bytes 1572872 | tf_op jit(solution)/shard_map/ppermute | solution.py:12
  180.0 2.3 fusion.155
  182.3 1.8 copy.191
  184.1 1.8 copy.188
  185.9 1.9 fusion.148
  189.7 5.0 %collective-permute-start.12 = (bf16[128,2048]{1,0:T(8,128)(2,1)}, bf16[128,2048]{1,0:T(8,128)(2,1)}, u32[]{:S(2)}, u32[]{:S(2)}) collective-permute-start(bf16[128,2048]{1,0:T(8,128)(2,1)} %collective-permute-done.10), channel_id=1, source_target_pairs={{0,8},{8,16},{16,24},{24,32},{32,40},{40,48},{48,56},{56,64},{64,7... | collective-permute-start | bytes 1572872 | tf_op jit(solution)/shard_map/ppermute | solution.py:12
  194.7 2.4 fusion.152
  197.0 1.9 collective-permute-start.13
  199.0 1.9 fusion.137
  200.8 1.8 copy.193
  206.2 2.3 fusion.153
  208.5 1.9 fusion.136
  212.2 1.9 fusion.149
  232.5 2.3 convolution_convert_fusion.1
  234.8 27.8 %all_to_all.10 = bf16[32,4,1280]{2,1,0:T(4,128)(2,1)S(1)} all-to-all(bf16[32,4,1280]{2,1,0:T(4,128)(2,1)S(1)} %reshape.1005), channel_id=1, replica_groups=mesh['grp'=32,'rep'=8] {'grp'}, dimensions={0} | all-to-all | bytes 655360 | tf_op jit(solution)/shard_map/all_to_all | solution.py:100
  (160 shorter events, 64.0 us)
Async XLA Ops:
  6.5 5.1 %copy-start = (bf16[1,64,1280]{2,1,0:T(8,128)(2,1)S(1)}, bf16[1,64,1280]{2,1,0:T(8,128)(2,1)}, u32[]{:S(2)}) copy-start(bf16[1,64,1280]{2,1,0:T(8,128)(2,1)} %param.6) | copy-start | bytes 491524
  6.5 18.2 %copy-start.24 = (s32[1,32]{1,0:T(1,128)S(1)}, s32[1,32]{1,0:T(1,128)}, u32[]{:S(2)}) copy-start(s32[1,32]{1,0:T(1,128)} %param.8) | copy-start | bytes 388
  6.5 60.6 %all-gather.3.cloned.1.call-start = ((), (), s32[]{:S(2)}) async-start(), calls=%async_computation.2 | async-start | bytes 8847360 | tf_op jit(solution)/shard_map/all_gather | solution.py:50
  7.3 59.9 %copy-start.25 = (f32[1280]{0:T(1024)S(1)}, f32[1280]{0:T(1024)}, u32[]{:S(2)}) copy-start(f32[1280]{0:T(1024)} %param.9) | copy-start | bytes 15364
  12.7 53.5 %all-to-all-start = ((bf16[32,4,1280]{2,1,0:T(4,128)(2,1)}), bf16[32,4,1280]{2,1,0:T(4,128)(2,1)S(1)}, u32[]{:S(2)}, u32[]{:S(2)}) async-start(bf16[32,4,1280]{2,1,0:T(4,128)(2,1)} %reshape.973), calls=%async_computation | async-start | bytes 655360 | tf_op jit(solution)/shard_map/all_to_all | solution.py:41
  23.9 208.6 %all-gather.5.cloned.1.call-start = ((), (), s32[]{:S(2)}) async-start(), calls=%async_computation.3 | async-start | bytes 2949120 | tf_op jit(solution)/shard_map/all_gather | solution.py:97
  72.5 12.5 %collective-permute-start.1 = (bf16[128,2048]{1,0:T(8,128)(2,1)}, bf16[128,2048]{1,0:T(8,128)(2,1)}, u32[]{:S(2)}, u32[]{:S(2)}) collective-permute-start(bf16[128,2048]{1,0:T(8,128)(2,1)} %slice.133), channel_id=1, source_target_pairs={{8,0},{16,8},{24,16},{32,24},{40,32},{48,40},{56,48},{64,56},{72,6... | collective-permute-start | bytes 1572872 | tf_op jit(solution)/shard_map/ppermute | solution.py:12
  76.0 13.5 %collective-permute-start = (bf16[128,2048]{1,0:T(8,128)(2,1)}, bf16[128,2048]{1,0:T(8,128)(2,1)}, u32[]{:S(2)}, u32[]{:S(2)}) collective-permute-start(bf16[128,2048]{1,0:T(8,128)(2,1)} %slice.133), channel_id=1, source_target_pairs={{0,8},{8,16},{16,24},{24,32},{32,40},{40,48},{48,56},{56,64},{64,7... | collective-permute-start | bytes 1572872 | tf_op jit(solution)/shard_map/ppermute | solution.py:12
  86.3 13.1 %collective-permute-start.3 = (bf16[128,2048]{1,0:T(8,128)(2,1)}, bf16[128,2048]{1,0:T(8,128)(2,1)}, u32[]{:S(2)}, u32[]{:S(2)}) collective-permute-start(bf16[128,2048]{1,0:T(8,128)(2,1)} %collective-permute-done.1), channel_id=1, source_target_pairs={{8,0},{16,8},{24,16},{32,24},{40,32},{48,40},{56,48},{64,56},{72,6... | collective-permute-start | bytes 1572872 | tf_op jit(solution)/shard_map/ppermute | solution.py:12
  89.4 12.9 %collective-permute-start.2 = (bf16[128,2048]{1,0:T(8,128)(2,1)}, bf16[128,2048]{1,0:T(8,128)(2,1)}, u32[]{:S(2)}, u32[]{:S(2)}) collective-permute-start(bf16[128,2048]{1,0:T(8,128)(2,1)} %collective-permute-done), channel_id=1, source_target_pairs={{0,8},{8,16},{16,24},{24,32},{32,40},{40,48},{48,56},{56,64},{64,7... | collective-permute-start | bytes 1572872 | tf_op jit(solution)/shard_map/ppermute | solution.py:12
  106.0 12.5 %collective-permute-start.5 = (bf16[128,2048]{1,0:T(8,128)(2,1)}, bf16[128,2048]{1,0:T(8,128)(2,1)}, u32[]{:S(2)}, u32[]{:S(2)}) collective-permute-start(bf16[128,2048]{1,0:T(8,128)(2,1)} %collective-permute-done.3), channel_id=1, source_target_pairs={{8,0},{16,8},{24,16},{32,24},{40,32},{48,40},{56,48},{64,56},{72,6... | collective-permute-start | bytes 1572872 | tf_op jit(solution)/shard_map/ppermute | solution.py:12
  109.6 19.2 %collective-permute-start.4 = (bf16[128,2048]{1,0:T(8,128)(2,1)}, bf16[128,2048]{1,0:T(8,128)(2,1)}, u32[]{:S(2)}, u32[]{:S(2)}) collective-permute-start(bf16[128,2048]{1,0:T(8,128)(2,1)} %collective-permute-done.2), channel_id=1, source_target_pairs={{0,8},{8,16},{16,24},{24,32},{32,40},{40,48},{48,56},{56,64},{64,7... | collective-permute-start | bytes 1572872 | tf_op jit(solution)/shard_map/ppermute | solution.py:12
  122.2 18.3 %collective-permute-start.7 = (bf16[128,2048]{1,0:T(8,128)(2,1)}, bf16[128,2048]{1,0:T(8,128)(2,1)}, u32[]{:S(2)}, u32[]{:S(2)}) collective-permute-start(bf16[128,2048]{1,0:T(8,128)(2,1)} %collective-permute-done.5), channel_id=1, source_target_pairs={{8,0},{16,8},{24,16},{32,24},{40,32},{48,40},{56,48},{64,56},{72,6... | collective-permute-start | bytes 1572872 | tf_op jit(solution)/shard_map/ppermute | solution.py:12
  128.8 15.3 %collective-permute-start.6 = (bf16[128,2048]{1,0:T(8,128)(2,1)}, bf16[128,2048]{1,0:T(8,128)(2,1)}, u32[]{:S(2)}, u32[]{:S(2)}) collective-permute-start(bf16[128,2048]{1,0:T(8,128)(2,1)} %collective-permute-done.4), channel_id=1, source_target_pairs={{0,8},{8,16},{16,24},{24,32},{32,40},{40,48},{48,56},{56,64},{64,7... | collective-permute-start | bytes 1572872 | tf_op jit(solution)/shard_map/ppermute | solution.py:12
  147.8 15.3 %collective-permute-start.9 = (bf16[128,2048]{1,0:T(8,128)(2,1)}, bf16[128,2048]{1,0:T(8,128)(2,1)}, u32[]{:S(2)}, u32[]{:S(2)}) collective-permute-start(bf16[128,2048]{1,0:T(8,128)(2,1)} %collective-permute-done.7), channel_id=1, source_target_pairs={{8,0},{16,8},{24,16},{32,24},{40,32},{48,40},{56,48},{64,56},{72,6... | collective-permute-start | bytes 1572872 | tf_op jit(solution)/shard_map/ppermute | solution.py:12
  152.3 21.1 %collective-permute-start.8 = (bf16[128,2048]{1,0:T(8,128)(2,1)}, bf16[128,2048]{1,0:T(8,128)(2,1)}, u32[]{:S(2)}, u32[]{:S(2)}) collective-permute-start(bf16[128,2048]{1,0:T(8,128)(2,1)} %collective-permute-done.6), channel_id=1, source_target_pairs={{0,8},{8,16},{16,24},{24,32},{32,40},{40,48},{48,56},{56,64},{64,7... | collective-permute-start | bytes 1572872 | tf_op jit(solution)/shard_map/ppermute | solution.py:12
  166.8 19.1 %collective-permute-start.11 = (bf16[128,2048]{1,0:T(8,128)(2,1)}, bf16[128,2048]{1,0:T(8,128)(2,1)}, u32[]{:S(2)}, u32[]{:S(2)}) collective-permute-start(bf16[128,2048]{1,0:T(8,128)(2,1)} %collective-permute-done.9), channel_id=1, source_target_pairs={{8,0},{16,8},{24,16},{32,24},{40,32},{48,40},{56,48},{64,56},{72,6... | collective-permute-start | bytes 1572872 | tf_op jit(solution)/shard_map/ppermute | solution.py:12
  177.0 12.6 %collective-permute-start.10 = (bf16[128,2048]{1,0:T(8,128)(2,1)}, bf16[128,2048]{1,0:T(8,128)(2,1)}, u32[]{:S(2)}, u32[]{:S(2)}) collective-permute-start(bf16[128,2048]{1,0:T(8,128)(2,1)} %collective-permute-done.8), channel_id=1, source_target_pairs={{0,8},{8,16},{16,24},{24,32},{32,40},{40,48},{48,56},{56,64},{64,7... | collective-permute-start | bytes 1572872 | tf_op jit(solution)/shard_map/ppermute | solution.py:12
  189.7 18.8 %collective-permute-start.12 = (bf16[128,2048]{1,0:T(8,128)(2,1)}, bf16[128,2048]{1,0:T(8,128)(2,1)}, u32[]{:S(2)}, u32[]{:S(2)}) collective-permute-start(bf16[128,2048]{1,0:T(8,128)(2,1)} %collective-permute-done.10), channel_id=1, source_target_pairs={{0,8},{8,16},{16,24},{24,32},{32,40},{40,48},{48,56},{56,64},{64,7... | collective-permute-start | bytes 1572872 | tf_op jit(solution)/shard_map/ppermute | solution.py:12
  197.0 15.2 %collective-permute-start.13 = (bf16[128,2048]{1,0:T(8,128)(2,1)}, bf16[128,2048]{1,0:T(8,128)(2,1)}, u32[]{:S(2)}, u32[]{:S(2)}) collective-permute-start(bf16[128,2048]{1,0:T(8,128)(2,1)} %collective-permute-done.11), channel_id=1, source_target_pairs={{8,0},{16,8},{24,16},{32,24},{40,32},{48,40},{56,48},{64,56},{72,6... | collective-permute-start | bytes 1572872 | tf_op jit(solution)/shard_map/ppermute | solution.py:12
  219.4 2.9 %copy-start.6 = (f32[16,128,128]{1,2,0:T(8,128)S(1)}, f32[16,128,128]{1,2,0:T(8,128)}, u32[]{:S(2)}) copy-start(f32[16,128,128]{1,2,0:T(8,128)} %get-tuple-element.133) | copy-start | bytes 3145732
  219.4 3.2 %copy-start.1 = (f32[16,128,128]{1,2,0:T(8,128)S(1)}, f32[16,128,128]{1,2,0:T(8,128)}, u32[]{:S(2)}) copy-start(f32[16,128,128]{1,2,0:T(8,128)} %get-tuple-element.125) | copy-start | bytes 3145732
  219.4 3.3 %copy-start.7 = (f32[16,128,128]{1,2,0:T(8,128)S(1)}, f32[16,128,128]{1,2,0:T(8,128)}, u32[]{:S(2)}) copy-start(f32[16,128,128]{1,2,0:T(8,128)} %get-tuple-element.127) | copy-start | bytes 3145732
  222.2 1.2 copy-start.2
  222.2 1.5 copy-start.8
  222.7 1.5 copy-start.3
  222.7 1.8 copy-start.9
  223.1 1.8 copy-start.4
  223.1 2.2 copy-start.10
  224.1 1.4 copy-start.5
  224.2 1.7 copy-start.11
  226.2 1.0 copy-start.12
  226.7 1.0 copy-start.13
  227.0 1.0 copy-start.14
  227.3 1.0 copy-start.15
  227.7 1.0 copy-start.16
  228.3 1.0 copy-start.17
  228.9 1.0 copy-start.18
  229.2 1.0 copy-start.19
  229.9 1.0 copy-start.20
  230.2 1.0 copy-start.21
  230.9 1.0 copy-start.22
  231.2 1.0 copy-start.23
Sparse Core Ops, SparseCore 0:
  9.2 52.5 all-gather.2
  63.7 28.9 all-gather.4
where the time goes:
time: 273 us; the launch traced here: 270 us
  local copies, waits for them, and re-layouts  78 us (29%)
  starting transfers between devices  56.7 us (21%)
  blocking collectives  48 us (18%)
  matrix products  40.1 us (15%)
  between operations  33.5 us (12%)
  other arithmetic  7.37 us (3%)
  waiting for transfers between devices  6.81 us (2%)
    slice x29, local copies, waits for them, and re-layouts, absorb(): vals = pair[:, inner:].reshape(slots, heads, HEAD_DIM)  46.5 us
    ppermute x14, starting transfers between devices, shifted(): return lax.ppermute(shard, axis, pairs)  45.5 us
    dot_general x15, matrix products, absorb(): jnp.einsum('shd,khd->hsk', query, keys, preferred_element_type=jnp.float32)  27.9 us
    all_to_all x1, blocking collectives, shards(): lax.all_to_all(projected.reshape(count, cap, width), 'grp', split_axis=0,...  27.8 us
    slice x16, local copies, waits for them, and re-layouts, absorb(): keys = pair[:, :inner].reshape(slots, heads, HEAD_DIM)  23.9 us
    unnamed x1, blocking collectives  20.2 us
    all_to_all x1, starting transfers between devices, shards(): lax.all_to_all(outgoing.reshape(count, cap, width), 'grp', split_axis=0,...  11.2 us
  transfers between devices with their start and end apart: 17, of which 2 were waited for; matrix products, arithmetic and copies ran while one was open for 44% of the time, Pallas kernels for 0%

commit v1 on v0

v1 whole, which is shorter than its diff:
```python
import math

import jax
import jax.numpy as jnp
from jax import lax
from jax.experimental import pallas as pl
from jax.experimental.pallas import tpu as pltpu
from jax.sharding import PartitionSpec as P

MESH = pl.DeviceIdType.MESH
NT = (((1,), (1,)), ((), ()))
BF = jnp.bfloat16
F32 = jnp.float32
D = 1280
ROWS = 64
HALF = 32
FR, DE, PL, GA, WL, WOL = 0, 1, 2, 3, 4, 5
XS, XR = 6, 10
WS, WR = 14, 15
OS, OR = 16, 20
FS, FRV = 24, 25
SBS = 26
QR = 27
GS, GR = 30, 31
PS, PR = 32, 35
CS, CR = 38, 39
NSEM = 40


def halves(block):
    return jnp.concatenate([block[:, 64:], block[:, :64]], axis=1)


def kernel(
    frames, dest, plan, gain, w_qkv, w_out, out,
    raw, dest_v, plan_v, gain_v, xb, w, wo, sb, own_g, rb, gb, vd, co, cb, spare,
    sem, line_x, line_s, line_y,
):
    g = lax.axis_index("grp")
    r = lax.axis_index("rep")
    x, z = lax.div(g, 8), lax.rem(g, 8)
    y, c = lax.div(r, 2), lax.rem(r, 2)
    cls = lax.rem(z, 2)
    slot = lax.div(z, 2) * 4 + x

    def at(tx, ty, tz, tc):
        return (tx * 8 + tz, ty * 2 + tc)

    def along_x(i):
        return at(lax.rem(x + i, 4), y, z, c)

    def along_y(i):
        return at(x, lax.rem(y + i, 4), z, c)

    sibling = at(x, y, z, 1 - c)

    def remote(src, dst, ssem, rsem, target):
        return pltpu.make_async_remote_copy(
            src_ref=src, dst_ref=dst, send_sem=sem.at[ssem], recv_sem=sem.at[rsem],
            device_id=target, device_id_type=MESH,
        )

    def local(src, dst, s):
        return pltpu.make_async_copy(src, dst, sem.at[s])

    def push(src, dst, ssem, rsem, tx, ty, tz, tc, dummy):
        same = (tx == x) & (ty == y) & (tz == z) & (tc == c)

        @pl.when(jnp.logical_not(same))
        def _():
            remote(src, dst, ssem, rsem, at(tx, ty, tz, tc)).start()

        @pl.when(same)
        def _():
            local(src, dst, rsem).start()
            local(src, spare.at[dummy], ssem).start()

    def drain(ref, s):
        local(ref, ref, s).wait()

    loads = [
        local(frames.at[0], raw, FR),
        local(dest.at[0], dest_v, DE),
        local(plan, plan_v, PL),
        local(gain, gain_v, GA),
        local(w_qkv, w.at[c], WL),
        local(w_out, wo.at[c, y], WOL),
    ]
    for load in loads:
        load.start()

    barrier = pltpu.get_barrier_semaphore()
    partners = [sibling] + [along_y(i) for i in (1, 2, 3)] + [along_x(i) for i in (1, 2, 3)]
    partners += [at(x, y, lax.rem(z + i, 8), c) for i in range(1, 8)]
    for partner in partners:
        pl.semaphore_signal(barrier, inc=1, device_id=partner, device_id_type=MESH)

    loads[0].wait()
    loads[3].wait()
    values = raw[...].astype(F32)
    mean = jnp.mean(values, axis=1, keepdims=True)
    centered = values - mean
    variance = jnp.mean(centered * centered, axis=1, keepdims=True)
    xb[0] = (centered * lax.rsqrt(variance + 1e-05) * gain_v[...]).astype(BF)

    pl.semaphore_wait(barrier, len(partners))

    for i in (1, 3, 2):
        remote(xb.at[0], xb.at[i], XS + i, XR + i, along_y(4 - i)).start()
    remote(w_qkv, w.at[c], WS, WR, sibling).start()
    for i in (1, 2, 3):
        pl.semaphore_signal(line_x, inc=1, device_id=along_x(i), device_id_type=MESH)

    loads[1].wait()
    loads[2].wait()
    hot = dest_v[...] == lax.broadcasted_iota(jnp.int32, (ROWS, 32), 1)
    group = jnp.sum(jnp.where(hot, plan_v[...].astype(F32), 0.0), axis=1, keepdims=True)
    low = lax.broadcasted_iota(jnp.int32, (1, 128), 1) < 64
    own_g[...] = jnp.where(low, group[:HALF], group[HALF:]).astype(BF)

    def project(i):
        block = xb[i]
        for s in range(2):
            part = jnp.dot(block, w[s], preferred_element_type=F32)
            for p in range(3):
                two = part[:, 128 * p : 128 * p + 128]
                top, bottom = two[:HALF], two[HALF:]
                sb[i, 6 * s + 2 * p] = jnp.where(low, top, halves(bottom)).astype(BF)
                sb[i, 6 * s + 2 * p + 1] = jnp.where(low, halves(top), bottom).astype(BF)

    def scatter(i):
        tz = lax.rem(y + i, 4) + 4 * c

        def one(j, carry):
            sub = 3 * y + lax.div(j, 4)
            kind, block = lax.div(sub, 4), lax.rem(sub, 4)
            ty = block + 1 - 2 * lax.rem(block, 2)
            push(
                sb.at[i, j], rb.at[kind, cls, pl.ds(slot * HALF, HALF)], SBS, QR + kind,
                lax.rem(j, 4), ty, tz, cls, 0,
            )
            return carry

        lax.fori_loop(0, 12, one, 0)

    loads[4].wait()
    remote(w_qkv, w.at[1 - c], WS, WR, sibling).wait_recv()
    project(0)

    pl.semaphore_wait(line_x, 3)
    pl.semaphore_signal(line_s, inc=1, device_id=sibling, device_id_type=MESH)
    pl.semaphore_wait(line_s, 1)
    for i in (1, 2, 3):
        pl.semaphore_signal(line_y, inc=1, device_id=along_y(i), device_id_type=MESH)
    pl.semaphore_wait(line_y, 3)

    def tell(j, carry):
        push(
            own_g, gb.at[cls, pl.ds(slot * HALF, HALF)], GS, GR,
            lax.rem(j, 4), lax.div(j, 4), y + 4 * c, cls, 1,
        )
        return carry

    lax.fori_loop(0, 16, tell, 0)
    scatter(0)
    for i in (1, 3, 2):
        remote(xb.at[0], xb.at[i], XS + i, XR + i, along_y(4 - i)).wait_recv()
        project(i)
        scatter(i)
    loads[5].wait()
    for i in (1, 3, 2):
        remote(
            wo.at[c, y], wo.at[c, y], OS + i, OR + i, along_y(4 - i)
        ).start()

    mine = [rb.at[1, c], rb.at[2, c], gb.at[c]]
    theirs = [rb.at[1, 1 - c], rb.at[2, 1 - c], gb.at[1 - c]]
    for n, s in enumerate((QR + 1, QR + 2, GR)):
        drain(mine[n], s)
        remote(mine[n], mine[n], PS + n, PR + n, sibling).start()
    drain(rb.at[0, c], QR)
    for n in range(3):
        drain(theirs[n], PR + n)

    first = lax.broadcasted_iota(jnp.int32, (8, 128), 1)
    groups = gb[...].reshape(1024, 128)
    key_low = lax.dot_general(
        jnp.where(first == 0, 1.0, 0.0).astype(BF), groups, NT, preferred_element_type=F32
    )[0:1]
    key_high = lax.dot_general(
        jnp.where(first == 64, 1.0, 0.0).astype(BF), groups, NT, preferred_element_type=F32
    )[0:1]
    vals = rb[2].reshape(1024, 128)
    vals_turned = halves(vals)
    vd[0:1024, :] = jnp.where(low, vals, vals_turned)
    vd[1024:2048, :] = jnp.where(low, vals_turned, vals)
    head = (y + 1 - 2 * lax.rem(y, 2)) * 4 + x
    owner_y, owner_c = lax.rem(z, 4), lax.div(z, 4)
    scale = 0.125 * math.log2(math.e)

    def attend(n, carry):
        m = lax.rem(lax.div(z, 2) + 2 + n * 3, 4)
        rows = pl.ds(pl.multiple_of(m * 128, 128), 128)
        q = rb[0, c, rows, :]
        turned = halves(q)
        none = jnp.zeros_like(q)
        q_low = jnp.concatenate([jnp.where(low, q, none), jnp.where(low, turned, none)], axis=0)
        q_high = jnp.concatenate([jnp.where(low, none, turned), jnp.where(low, none, q)], axis=0)
        gq = gb[c, rows, :].astype(F32)
        gq = jnp.concatenate([gq[:, 0:1], gq[:, 64:65]], axis=0)
        keys = rb[1].reshape(1024, 128)
        s_low = lax.dot_general(q_low, keys, NT, preferred_element_type=F32)
        s_high = lax.dot_general(q_high, keys, NT, preferred_element_type=F32)
        s_low = jnp.where(gq == key_low, s_low, -jnp.inf)
        s_high = jnp.where(gq == key_high, s_high, -jnp.inf)
        top = jnp.maximum(
            jnp.max(s_low, axis=1, keepdims=True), jnp.max(s_high, axis=1, keepdims=True)
        )
        p_low = jnp.exp2((s_low - top) * scale)
        p_high = jnp.exp2((s_high - top) * scale)
        total = jnp.sum(p_low, axis=1, keepdims=True) + jnp.sum(p_high, axis=1, keepdims=True)
        context = jnp.dot(p_low.astype(BF), vd[0:1024, :], preferred_element_type=F32)
        context += jnp.dot(p_high.astype(BF), vd[1024:2048, :], preferred_element_type=F32)
        context = context / total
        co[rows, :] = jnp.where(low, context[:128], context[128:]).astype(BF)
        for i in range(4):
            push(
                co.at[pl.ds(m * 128 + HALF * i, HALF)],
                cb.at[lax.div(x, 2), lax.div(head, 4), lax.rem(x, 2)],
                CS, CR, i, owner_y, 2 * m + c, owner_c, 2,
            )
        return carry

    lax.fori_loop(0, 4, attend, 0)

    for i in (1, 2, 3):
        remote(wo.at[c, y], wo.at[c, lax.rem(y + i, 4)], OS + i, OR + i, along_y(4 - i)).wait_recv()
    remote(wo.at[c], wo.at[c], FS, FRV, sibling).start()

    drain(cb, CR)
    pieces = []
    for tc in range(2):
        for ty in range(4):
            even, odd = cb[tc, ty, 0], cb[tc, ty, 1]
            pieces.append(
                jnp.concatenate(
                    [jnp.where(low, even, halves(odd)), jnp.where(low, halves(even), odd)], axis=0
                )
            )
    context = jnp.concatenate(pieces, axis=1)
    remote(wo.at[c], wo.at[1 - c], FS, FRV, sibling).wait_recv()
    for n in range(5):
        cols = slice(256 * n, 256 * n + 256)
        weights = wo[:, :, :, cols].reshape(1024, 256)
        out[0, :, cols] = jnp.dot(context, weights, preferred_element_type=F32).astype(BF)

    for i in (1, 2, 3):
        remote(xb.at[0], xb.at[i], XS + i, XR + i, along_y(4 - i)).wait_send()
        remote(wo.at[c, y], wo.at[c, y], OS + i, OR + i, along_y(4 - i)).wait_send()
    remote(w_qkv, w.at[c], WS, WR, sibling).wait_send()
    remote(wo.at[c], wo.at[c], FS, FRV, sibling).wait_send()
    drain(sb, SBS)
    for n in range(3):
        remote(mine[n], mine[n], PS + n, PR + n, sibling).wait_send()
    drain(gb.at[c], GS)
    drain(co, CS)


def shards(frames, destination, plan, norm_gain, w_qkv, w_out):
    any_space = pl.BlockSpec(memory_space=pl.ANY)
    return pl.pallas_call(
        kernel,
        out_shape=jax.ShapeDtypeStruct((1, ROWS, D), BF),
        in_specs=[any_space] * 6,
        out_specs=pl.BlockSpec(memory_space=pltpu.VMEM),
        scratch_shapes=[
            pltpu.VMEM((ROWS, D), BF),
            pltpu.VMEM((ROWS, 1), jnp.int32),
            pltpu.VMEM((1, 32), jnp.int32),
            pltpu.VMEM((1, D), F32),
            pltpu.VMEM((4, ROWS, D), BF),
            pltpu.VMEM((2, D, 384), BF),
            pltpu.VMEM((2, 4, 128, D), BF),
            pltpu.VMEM((4, 12, HALF, 128), BF),
            pltpu.VMEM((HALF, 128), BF),
            pltpu.VMEM((3, 2, 512, 128), BF),
            pltpu.VMEM((2, 512, 128), BF),
            pltpu.VMEM((2048, 128), BF),
            pltpu.VMEM((512, 128), BF),
            pltpu.VMEM((2, 4, 2, HALF, 128), BF),
            pltpu.VMEM((3, HALF, 128), BF),
            pltpu.SemaphoreType.DMA((NSEM,)),
            pltpu.SemaphoreType.REGULAR,
            pltpu.SemaphoreType.REGULAR,
            pltpu.SemaphoreType.REGULAR,
        ],
        compiler_params=pltpu.CompilerParams(
            collective_id=0, has_side_effects=True, vmem_limit_bytes=48 * 2**20
        ),
        name="attend",
    )(frames, destination, plan, norm_gain.reshape(1, D), w_qkv, w_out)


def solution(mesh):
    in_specs = (
        P("rep", "grp", None),
        P("rep", "grp", None),
        P("rep", None),
        P(),
        P(None, "rep"),
        P("rep", None),
    )
    out_specs = P("rep", "grp", None)
    return jax.shard_map(shards, mesh=mesh, in_specs=in_specs, out_specs=out_specs, check_vma=False)
```

time: 273 us -> 51.2 us (0.19)
  the two profiles are of different devices: /device:TPU:32 before, /device:TPU:16 now
where the time goes in v1:
time: 51.2 us; the launch traced here: 50.9 us
  Pallas kernels  45.8 us (89%)
  local copies, waits for them, and re-layouts  5.13 us (10%)
    pallas_call x1, Pallas kernels, shards(): pl.pallas_call(kernel, out_shape=jax.ShapeDtypeStruct((1, ROWS, D), BF),...  45.8 us
    unnamed x12, local copies, waits for them, and re-layouts  4.41 us

profile of v1, /device:TPU:16, one launch (start us, length us, event | category | flops | bytes accessed | tf_op | source)
XLA Modules:
  0.0 50.9 jit_solution(4276909860436630027)
XLA Ops:
  0.0 0.0 copy-start.4
  0.0 0.7 %reshape.3.gain = f32[1,1280]{1,0:T(1,128)S(1)} reshape(f32[1280]{0:T(1024)} %param.9) | data formatting | bytes 10240 | tf_op jit(solution)/shard_map/reshape | solution.py:301
  0.7 0.0 copy-done.4
  0.7 0.0 copy-start.3
  0.7 0.1 copy.7.dest
  0.8 0.6 %copy-done.3 = s32[1,32]{1,0:T(1,128)S(1)} copy-done((s32[1,32]{1,0:T(1,128)S(1)}, s32[1,32]{1,0:T(1,128)}, u32[]{:S(2)}) %copy-start.3) | copy-done | bytes 152
  1.4 0.0 copy-start
  1.4 1.2 %copy-done = bf16[1280,384]{1,0:T(8,128)(2,1)S(1)} copy-done((bf16[1280,384]{1,0:T(8,128)(2,1)S(1)}, bf16[1280,384]{1,0:T(8,128)(2,1)}, u32[]{:S(2)}) %copy-start) | copy-done | bytes 983064
  2.6 0.0 copy-start.1
  2.6 1.0 %copy-done.1 = bf16[128,1280]{1,0:T(8,128)(2,1)S(1)} copy-done((bf16[128,1280]{1,0:T(8,128)(2,1)S(1)}, bf16[128,1280]{1,0:T(8,128)(2,1)}, u32[]{:S(2)}) %copy-start.1) | copy-done | bytes 327704
  3.6 0.0 copy-start.2
  3.6 0.9 %copy-done.2 = bf16[1,64,1280]{2,1,0:T(8,128)(2,1)S(1)} copy-done((bf16[1,64,1280]{2,1,0:T(8,128)(2,1)S(1)}, bf16[1,64,1280]{2,1,0:T(8,128)(2,1)}, u32[]{:S(2)}) %copy-start.2) | copy-done | bytes 163864
  4.5 45.8 %attend.1 = bf16[1,64,1280]{2,1,0:T(8,128)(2,1)S(1)} custom-call(bf16[1,64,1280]{2,1,0:T(8,128)(2,1)S(1)} %copy-done.2, s32[1,64,1]{2,1,0:T(8,128)S(1)} %copy.7.dest, s32[1,32]{1,0:T(1,128)S(1)} %copy-done.3, f32[1,1280]{1,0:T(1,128)S(1)} %reshape.3.gain, bf16[1280,384]{1,0:T(8,128)(2,1)S(1)} %copy-done, bf16[128,1280]{1,0:T(8,128)(2,1)S(1)} %copy-done.1), custom_call_target="tpu_custom_call" | custom-call | tf_op jit(solution)/shard_map/attend/pallas_call | solution.py:271
  50.3 0.7 %copy.9 = bf16[1,64,1280]{2,1,0:T(8,128)(2,1)} copy(bf16[1,64,1280]{2,1,0:T(8,128)(2,1)S(1)} %attend.1) | data formatting | bytes 327680
Async XLA Ops:
  0.0 0.7 %copy-start.4 = (s32[1,64,1]{1,2,0:T(1,128)S(1)}, s32[1,64,1]{1,2,0:T(1,128)}, u32[]{:S(2)}) copy-start(s32[1,64,1]{1,2,0:T(1,128)} %param.7) | copy-start | bytes 772
  0.7 0.7 %copy-start.3 = (s32[1,32]{1,0:T(1,128)S(1)}, s32[1,32]{1,0:T(1,128)}, u32[]{:S(2)}) copy-start(s32[1,32]{1,0:T(1,128)} %plan.1) | copy-start | bytes 388
  1.4 1.2 %copy-start = (bf16[1280,384]{1,0:T(8,128)(2,1)S(1)}, bf16[1280,384]{1,0:T(8,128)(2,1)}, u32[]{:S(2)}) copy-start(bf16[1280,384]{1,0:T(8,128)(2,1)} %w_qkv.1) | copy-start | bytes 2949124
  2.6 1.0 %copy-start.1 = (bf16[128,1280]{1,0:T(8,128)(2,1)S(1)}, bf16[128,1280]{1,0:T(8,128)(2,1)}, u32[]{:S(2)}) copy-start(bf16[128,1280]{1,0:T(8,128)(2,1)} %w_out.1) | copy-start | bytes 983044
  3.6 0.9 %copy-start.2 = (bf16[1,64,1280]{2,1,0:T(8,128)(2,1)S(1)}, bf16[1,64,1280]{2,1,0:T(8,128)(2,1)}, u32[]{:S(2)}) copy-start(bf16[1,64,1280]{2,1,0:T(8,128)(2,1)} %frames.1) | copy-start | bytes 491524

commit v2 on v1

v2 whole, which is shorter than its diff:
```python
import math

import jax
import jax.numpy as jnp
from jax import lax
from jax.experimental import pallas as pl
from jax.experimental.pallas import tpu as pltpu
from jax.sharding import PartitionSpec as P

MESH = pl.DeviceIdType.MESH
NT = (((1,), (1,)), ((), ()))
BF = jnp.bfloat16
F32 = jnp.float32
D = 1280
ROWS = 64
HALF = 32
FR, DE, PL, GA, WL, WOL = 0, 1, 2, 3, 4, 5
XS, XR = 6, 10
WS, WR = 14, 15
OS, OR = 16, 20
FS, FT = 24, 28
SBS = 32
QR = 33
GS, GR = 36, 37
PS, PR = 38, 41
CS, CR = 44, 45
NSEM = 46


def halves(block):
    return jnp.concatenate([block[:, 64:], block[:, :64]], axis=1)


def kernel(
    frames, dest, plan, gain, w_qkv, w_out, out,
    raw, dest_v, plan_v, gain_v, xb, w, wo, sb, own_g, rb, gb, vd, co, cb, acc, top_v, sum_v,
    spare, spare_g, sem, line_x, line_y,
):
    g = lax.axis_index("grp")
    r = lax.axis_index("rep")
    x, z = lax.div(g, 8), lax.rem(g, 8)
    y, c = lax.div(r, 2), lax.rem(r, 2)
    cls = lax.rem(z, 2)
    slot = lax.div(z, 2) * 4 + x

    def at(tx, ty, tz, tc):
        return (tx * 8 + tz, ty * 2 + tc)

    def turn_x(i):
        return lax.rem(x + i, 4)

    def along_y(i):
        return at(x, lax.rem(y + i, 4), z, c)

    sibling = at(x, y, z, 1 - c)

    def remote(src, dst, ssem, rsem, target):
        return pltpu.make_async_remote_copy(
            src_ref=src, dst_ref=dst, send_sem=sem.at[ssem], recv_sem=sem.at[rsem],
            device_id=target, device_id_type=MESH,
        )

    def local(src, dst, s):
        return pltpu.make_async_copy(src, dst, sem.at[s])

    def push(src, dst, ssem, rsem, tx, ty, tz, tc, dummy):
        if dummy is None:
            remote(src, dst, ssem, rsem, at(tx, ty, tz, tc)).start()
            return
        same = (ty == y) & (tz == z) & (tc == c)

        @pl.when(jnp.logical_not(same))
        def _():
            remote(src, dst, ssem, rsem, at(tx, ty, tz, tc)).start()

        @pl.when(same)
        def _():
            local(src, dst, rsem).start()
            local(src, dummy, ssem).start()

    def drain(ref, s):
        local(ref, ref, s).wait()

    loads = [
        local(frames.at[0], raw, FR),
        local(dest, dest_v, DE),
        local(plan, plan_v, PL),
        local(gain, gain_v, GA),
        local(w_qkv, w.at[c], WL),
        local(w_out, wo.at[c, y], WOL),
    ]
    for load in loads:
        load.start()

    barrier = pltpu.get_barrier_semaphore()
    plane = [at(turn_x(i), y, z, c) for i in (1, 2, 3)]
    plane += [at(turn_x(i), y, z, 1 - c) for i in range(4)]
    partners = [along_y(i) for i in (1, 2, 3)] + plane
    partners += [at(x, y, lax.rem(z + i, 8), c) for i in range(1, 8)]
    for partner in partners:
        pl.semaphore_signal(barrier, inc=1, device_id=partner, device_id_type=MESH)

    low = lax.broadcasted_iota(jnp.int32, (1, 128), 1) < 64
    loads[1].wait()
    loads[2].wait()
    row32 = lax.broadcasted_iota(jnp.int32, (32, 32), 0)
    col32 = lax.broadcasted_iota(jnp.int32, (32, 32), 1)
    plan_rows = jnp.sum(
        jnp.where(row32 == col32, plan_v[...].astype(F32), 0.0), axis=1, keepdims=True
    )
    hot = dest_v[...] == lax.broadcasted_iota(jnp.int32, (32, ROWS), 0)
    group = jnp.sum(jnp.where(hot, plan_rows, 0.0), axis=0, keepdims=True)
    own_g[...] = jnp.concatenate([group, group], axis=1)

    loads[0].wait()
    loads[3].wait()
    values = raw[...].astype(F32)
    mean = jnp.mean(values, axis=1, keepdims=True)
    centered = values - mean
    variance = jnp.mean(centered * centered, axis=1, keepdims=True)
    xb[0] = (centered * lax.rsqrt(variance + 1e-05) * gain_v[...][None, :]).astype(BF)

    pl.semaphore_wait(barrier, len(partners))

    for i in (1, 3, 2):
        remote(xb.at[0], xb.at[i], XS + i, XR + i, along_y(4 - i)).start()
    remote(w_qkv, w.at[c], WS, WR, sibling).start()
    for partner in plane:
        pl.semaphore_signal(line_x, inc=1, device_id=partner, device_id_type=MESH)

    def project(i, s):
        part = jnp.dot(xb[i], w[s], preferred_element_type=F32)
        for p in range(3):
            two = part[:, 128 * p : 128 * p + 128]
            upper, lower = two[:HALF], two[HALF:]
            sb[i, 6 * s + 2 * p] = jnp.where(low, upper, halves(lower)).astype(BF)
            sb[i, 6 * s + 2 * p + 1] = jnp.where(low, halves(upper), lower).astype(BF)

    def scatter(i):
        tz = lax.rem(y + i, 4) + 4 * c
        for s in range(3):
            sub = 3 * y + s
            kind, block = lax.div(sub, 4), lax.rem(sub, 4)
            ty = block + 1 - 2 * lax.rem(block, 2)
            for k in (2, 1, 3, 0):
                push(
                    sb.at[i, 4 * s + turn_x(k)], rb.at[kind, cls, pl.ds(slot * HALF, HALF)],
                    SBS, QR + kind, turn_x(k), ty, tz, cls, None if k else spare.at[0],
                )

    loads[4].wait()
    project(0, c)
    pl.semaphore_wait(line_x, len(plane))
    for i in (1, 2, 3):
        pl.semaphore_signal(line_y, inc=1, device_id=along_y(i), device_id_type=MESH)
    remote(w_qkv, w.at[1 - c], WS, WR, sibling).wait_recv()
    project(0, 1 - c)
    pl.semaphore_wait(line_y, 3)

    scatter(0)
    for k in (2, 1, 3, 0):
        for i in (2, 1, 3, 0):
            push(
                own_g, gb.at[cls, slot], GS, GR, turn_x(k), lax.rem(y + i, 4), y + 4 * c, cls,
                None if k or i else spare_g,
            )
    for i in (1, 3, 2):
        remote(xb.at[0], xb.at[i], XS + i, XR + i, along_y(4 - i)).wait_recv()
        project(i, 0)
        project(i, 1)
        scatter(i)
    loads[5].wait()
    for i in (1, 3, 2):
        remote(wo.at[c, y], wo.at[c, y], OS + i, OR + i, along_y(4 - i)).start()

    def to_sibling(i):
        ty = lax.rem(y + i, 4)
        return remote(wo.at[c, ty], wo.at[c, ty], FS + i, FT + i, sibling)

    to_sibling(0).start()

    mine = [rb.at[1, c], rb.at[2, c], gb.at[c]]
    theirs = [rb.at[1, 1 - c], rb.at[2, 1 - c], gb.at[1 - c]]
    for n, s in ((2, GR), (0, QR + 1), (1, QR + 2)):
        drain(mine[n], s)
        remote(mine[n], mine[n], PS + n, PR + n, sibling).start()
    drain(rb.at[0, c], QR)

    lane = lax.broadcasted_iota(jnp.int32, (1, 512), 1)
    depth = lax.broadcasted_iota(jnp.int32, (128, 512), 0)
    source = lax.broadcasted_iota(jnp.int32, (16, 512), 0) == lax.div(lane, HALF)

    def key_groups(half):
        table = jnp.concatenate([gb[half, n] for n in range(16)], axis=0).astype(BF)
        both = []
        for base in (0, HALF):
            spread = jnp.where(depth == lax.rem(lane, HALF) + base, 1.0, 0.0).astype(BF)
            wide = jnp.dot(table, spread, preferred_element_type=F32)
            both.append(jnp.sum(jnp.where(source, wide, 0.0), axis=0, keepdims=True))
        return both

    def spread_values(half):
        vals = rb[2, half]
        turned = halves(vals)
        vd[half, 0:512, :] = jnp.where(low, vals, turned)
        vd[half, 512:1024, :] = jnp.where(low, turned, vals)

    head = (y + 1 - 2 * lax.rem(y, 2)) * 4 + x
    owner_y, owner_c = lax.rem(z, 4), lax.div(z, 4)
    scale = 0.125 * math.log2(math.e)
    row = lax.rem(lax.broadcasted_iota(jnp.int32, (128, 128), 0), HALF)
    col = lax.broadcasted_iota(jnp.int32, (128, 128), 1)

    def chunk(n):
        return lax.rem(lax.div(z, 2) + 2 + n * 3, 4)

    def scores(m, half, key_low, key_high):
        rows = pl.ds(pl.multiple_of(m * 128, 128), 128)
        q = rb[0, c, rows, :]
        turned = halves(q)
        none = jnp.zeros_like(q)
        q_low = jnp.concatenate([jnp.where(low, q, none), jnp.where(low, turned, none)], axis=0)
        q_high = jnp.concatenate([jnp.where(low, none, turned), jnp.where(low, none, q)], axis=0)
        mine_g = jnp.concatenate(
            [jnp.broadcast_to(gb[c, 4 * m + n], (HALF, 128)) for n in range(4)], axis=0
        )
        gq = jnp.concatenate(
            [
                jnp.sum(jnp.where(col == row + base, mine_g, 0.0), axis=1, keepdims=True)
                for base in (0, HALF)
            ],
            axis=0,
        )
        keys = rb[1, half]
        s_low = lax.dot_general(q_low, keys, NT, preferred_element_type=F32)
        s_high = lax.dot_general(q_high, keys, NT, preferred_element_type=F32)
        s_low = jnp.where(gq == key_low, s_low, -jnp.inf)
        s_high = jnp.where(gq == key_high, s_high, -jnp.inf)
        top = jnp.maximum(
            jnp.max(s_low, axis=1, keepdims=True), jnp.max(s_high, axis=1, keepdims=True)
        )
        return s_low, s_high, top

    def weigh(s_low, s_high, top, half):
        p_low = jnp.exp2((s_low - top) * scale)
        p_high = jnp.exp2((s_high - top) * scale)
        total = jnp.sum(p_low, axis=1, keepdims=True) + jnp.sum(p_high, axis=1, keepdims=True)
        mixed = jnp.dot(p_low.astype(BF), vd[half, 0:512, :], preferred_element_type=F32)
        mixed += jnp.dot(p_high.astype(BF), vd[half, 512:1024, :], preferred_element_type=F32)
        return total, mixed

    key_low, key_high = key_groups(c)
    spread_values(c)

    def first_half(n, carry):
        s_low, s_high, top = scores(chunk(n), c, key_low, key_high)
        total, mixed = weigh(s_low, s_high, top, c)
        top_v[n] = top
        sum_v[n] = total
        acc[n] = mixed
        return carry

    lax.fori_loop(0, 4, first_half, 0)

    for n in range(3):
        drain(theirs[n], PR + n)
    other_low, other_high = key_groups(1 - c)
    spread_values(1 - c)

    def second_half(n, carry):
        m = chunk(n)
        s_low, s_high, top = scores(m, 1 - c, other_low, other_high)
        before = top_v[n]
        top = jnp.maximum(before, top)
        total, mixed = weigh(s_low, s_high, top, 1 - c)
        factor = jnp.exp2((before - top) * scale)
        context = (acc[n] * factor + mixed) / (sum_v[n] * factor + total)
        co[pl.ds(pl.multiple_of(m * 128, 128), 128), :] = jnp.where(
            low, context[:128], context[128:]
        ).astype(BF)
        for k in (2, 1, 3, 0):
            push(
                co.at[pl.ds(m * 128 + HALF * turn_x(k), HALF)],
                cb.at[lax.div(x, 2), lax.div(head, 4), lax.rem(x, 2)],
                CS, CR, turn_x(k), owner_y, 2 * m + c, owner_c, None if k else spare.at[1],
            )
        return carry

    lax.fori_loop(0, 4, second_half, 0)

    for i in (1, 3, 2):
        remote(wo.at[c, y], wo.at[c, lax.rem(y + i, 4)], OS + i, OR + i, along_y(4 - i)).wait_recv()
        to_sibling(i).start()

    drain(cb, CR)
    pieces = []
    for tc in range(2):
        for ty in range(4):
            even, odd = cb[tc, ty, 0], cb[tc, ty, 1]
            pieces.append(
                jnp.concatenate(
                    [jnp.where(low, even, halves(odd)), jnp.where(low, halves(even), odd)], axis=0
                )
            )
    context = jnp.concatenate(pieces, axis=1)
    for i in range(4):
        ty = lax.rem(y + i, 4)
        remote(wo.at[c, ty], wo.at[1 - c, ty], FS + i, FT + i, sibling).wait_recv()
    for n in range(5):
        cols = slice(256 * n, 256 * n + 256)
        weights = wo[:, :, :, cols].reshape(1024, 256)
        out[0, :, cols] = jnp.dot(context, weights, preferred_element_type=F32).astype(BF)

    for i in (1, 2, 3):
        remote(xb.at[0], xb.at[i], XS + i, XR + i, along_y(4 - i)).wait_send()
        remote(wo.at[c, y], wo.at[c, y], OS + i, OR + i, along_y(4 - i)).wait_send()
    remote(w_qkv, w.at[c], WS, WR, sibling).wait_send()
    for i in range(4):
        to_sibling(i).wait_send()
    drain(sb, SBS)
    for n in range(3):
        remote(mine[n], mine[n], PS + n, PR + n, sibling).wait_send()
    drain(gb.at[c], GS)
    drain(co, CS)


SCRATCH = [
    pltpu.VMEM((ROWS, D), BF),
    pltpu.VMEM((1, ROWS), jnp.int32),
    pltpu.VMEM((1, 32), jnp.int32),
    pltpu.VMEM((D,), F32),
    pltpu.VMEM((4, ROWS, D), BF),
    pltpu.VMEM((2, D, 384), BF),
    pltpu.VMEM((2, 4, 128, D), BF),
    pltpu.VMEM((4, 12, HALF, 128), BF),
    pltpu.VMEM((1, 128), F32),
    pltpu.VMEM((3, 2, 512, 128), BF),
    pltpu.VMEM((2, 16, 1, 128), F32),
    pltpu.VMEM((2, 1024, 128), BF),
    pltpu.VMEM((512, 128), BF),
    pltpu.VMEM((2, 4, 2, HALF, 128), BF),
    pltpu.VMEM((4, 256, 128), F32),
    pltpu.VMEM((4, 256, 1), F32),
    pltpu.VMEM((4, 256, 1), F32),
    pltpu.VMEM((2, HALF, 128), BF),
    pltpu.VMEM((1, 128), F32),
    pltpu.SemaphoreType.DMA((NSEM,)),
    pltpu.SemaphoreType.REGULAR,
    pltpu.SemaphoreType.REGULAR,
]


def shards(frames, destination, plan, norm_gain, w_qkv, w_out):
    any_space = pl.BlockSpec(memory_space=pl.ANY)
    return pl.pallas_call(
        kernel,
        out_shape=jax.ShapeDtypeStruct((1, ROWS, D), BF),
        in_specs=[any_space] * 6,
        out_specs=pl.BlockSpec(memory_space=pltpu.VMEM),
        scratch_shapes=SCRATCH,
        compiler_params=pltpu.CompilerParams(
            collective_id=0, has_side_effects=True, vmem_limit_bytes=60 * 2**20
        ),
        name="attend",
    )(frames, destination.reshape(1, ROWS), plan, norm_gain, w_qkv, w_out)


def solution(mesh):
    in_specs = (
        P("rep", "grp", None),
        P("rep", "grp", None),
        P("rep", None),
        P(),
        P(None, "rep"),
        P("rep", None),
    )
    out_specs = P("rep", "grp", None)
    return jax.shard_map(shards, mesh=mesh, in_specs=in_specs, out_specs=out_specs, check_vma=False)
```

time: 51.2 us -> 44.3 us (0.87)
  the two profiles are of different devices: /device:TPU:16 before, /device:TPU:95 now
where the time goes in v2:
time: 44.3 us; the launch traced here: 44.2 us
  Pallas kernels  42.6 us (96%)
  local copies, waits for them, and re-layouts  1.59 us (4%)
    pallas_call x1, Pallas kernels, shards(): pl.pallas_call(kernel, out_shape=jax.ShapeDtypeStruct((1, ROWS, D), BF),...  42.6 us
    unnamed x1, local copies, waits for them, and re-layouts  1.59 us

profile of v2, /device:TPU:95, one launch (start us, length us, event | category | flops | bytes accessed | tf_op | source)
XLA Modules:
  0.0 44.2 jit_solution(8984077560208967900)
XLA Ops:
  0.0 42.6 %attend.1 = bf16[1,64,1280]{2,1,0:T(8,128)(2,1)} custom-call(bf16[1,64,1280]{2,1,0:T(8,128)(2,1)} %frames.1, s32[1,64]{1,0:T(1,128)} %bitcast.1, s32[1,32]{1,0:T(1,128)} %plan.1, f32[1280]{0:T(1024)} %gain.1, bf16[1280,384]{1,0:T(8,128)(2,1)} %w_qkv.1, bf16[128,1280]{1,0:T(8,128)(2,1)} %w_out.1), custom_call_target="tpu_custom_call" | custom-call | tf_op jit(solution)/shard_map/attend/pallas_call | solution.py:355
  42.6 1.6 %copy.8 = bf16[1,64,1280]{2,1,0:T(8,128)(2,1)} copy(bf16[1,64,1280]{2,1,0:T(8,128)(2,1)} %attend.1) | data formatting | bytes 327680

commit v3 on v2

--- a/solution.py
+++ b/solution.py
@@ -33,8 +33,8 @@
 
 def kernel(
     frames, dest, plan, gain, w_qkv, w_out, out,
-    raw, dest_v, plan_v, gain_v, xb, w, wo, sb, own_g, rb, gb, vd, co, cb, acc, top_v, sum_v,
-    spare, spare_g, sem, line_x, line_y,
+    raw, dest_v, plan_v, gain_v, xb, w, wo, sb, own_g, rb, gb, key_mark, query_mark, vd, co, cb, acc, top_v,
+    sum_v, spare, spare_g, sem, line_x, line_y,
 ):
     g = lax.axis_index("grp")
     r = lax.axis_index("rep")
@@ -181,23 +181,45 @@
 
     mine = [rb.at[1, c], rb.at[2, c], gb.at[c]]
     theirs = [rb.at[1, 1 - c], rb.at[2, 1 - c], gb.at[1 - c]]
-    for n, s in ((2, GR), (0, QR + 1), (1, QR + 2)):
+
+    def swap(n, s):
         drain(mine[n], s)
         remote(mine[n], mine[n], PS + n, PR + n, sibling).start()
+
+    lane = lax.broadcasted_iota(jnp.int32, (1, 128), 1)
+    lane_group = jnp.where(lane < 64, lax.rem(lax.div(lane, 4), 8), -1).astype(F32)
+    row = lax.rem(lax.broadcasted_iota(jnp.int32, (128, 128), 0), HALF)
+    col = lax.broadcasted_iota(jnp.int32, (128, 128), 1)
+
+    def group_columns(half, m):
+        table = jnp.concatenate(
+            [jnp.broadcast_to(gb[half, 4 * m + n], (HALF, 128)) for n in range(4)], axis=0
+        )
+        return [
+            jnp.sum(jnp.where(col == row + base, table, 0.0), axis=1, keepdims=True)
+            for base in (0, HALF)
+        ]
+
+    def mark_keys(half, m):
+        for_low, for_high = group_columns(half, m)
+        hit = jnp.where(lane < 32, for_low, for_high) == lane_group
+        key_mark[half, 128 * m : 128 * m + 128, :] = jnp.where(hit, 1.0, 0.0).astype(BF)
+        if half is not c:
+            return
+        group = jnp.concatenate([for_low, for_high], axis=0)
+        miss = jnp.where(group == lane_group, 0.0, -(2.0**127))
+        query_mark[0, m] = jnp.where(lane < 32, miss, 0.0).astype(BF)
+        query_mark[1, m] = jnp.where((lane >= 32) & (lane < 64), miss, 0.0).astype(BF)
+
+    swap(2, GR)
+    for m in range(4):
+        mark_keys(c, m)
+    drain(theirs[2], PR + 2)
+    for m in range(4):
+        mark_keys(1 - c, m)
+    swap(0, QR + 1)
+    swap(1, QR + 2)
     drain(rb.at[0, c], QR)
-
-    lane = lax.broadcasted_iota(jnp.int32, (1, 512), 1)
-    depth = lax.broadcasted_iota(jnp.int32, (128, 512), 0)
-    source = lax.broadcasted_iota(jnp.int32, (16, 512), 0) == lax.div(lane, HALF)
-
-    def key_groups(half):
-        table = jnp.concatenate([gb[half, n] for n in range(16)], axis=0).astype(BF)
-        both = []
-        for base in (0, HALF):
-            spread = jnp.where(depth == lax.rem(lane, HALF) + base, 1.0, 0.0).astype(BF)
-            wide = jnp.dot(table, spread, preferred_element_type=F32)
-            both.append(jnp.sum(jnp.where(source, wide, 0.0), axis=0, keepdims=True))
-        return both
 
     def spread_values(half):
         vals = rb[2, half]
@@ -208,38 +230,28 @@
     head = (y + 1 - 2 * lax.rem(y, 2)) * 4 + x
     owner_y, owner_c = lax.rem(z, 4), lax.div(z, 4)
     scale = 0.125 * math.log2(math.e)
-    row = lax.rem(lax.broadcasted_iota(jnp.int32, (128, 128), 0), HALF)
-    col = lax.broadcasted_iota(jnp.int32, (128, 128), 1)
 
     def chunk(n):
         return lax.rem(lax.div(z, 2) + 2 + n * 3, 4)
 
-    def scores(m, half, key_low, key_high):
-        rows = pl.ds(pl.multiple_of(m * 128, 128), 128)
-        q = rb[0, c, rows, :]
+    def scores(m, half):
+        q = rb[0, c, pl.ds(pl.multiple_of(m * 128, 128), 128), :]
         turned = halves(q)
         none = jnp.zeros_like(q)
         q_low = jnp.concatenate([jnp.where(low, q, none), jnp.where(low, turned, none)], axis=0)
         q_high = jnp.concatenate([jnp.where(low, none, turned), jnp.where(low, none, q)], axis=0)
-        mine_g = jnp.concatenate(
-            [jnp.broadcast_to(gb[c, 4 * m + n], (HALF, 128)) for n in range(4)], axis=0
+        keys = jnp.concatenate([rb[1, half], key_mark[half]], axis=1)
+        both = [
+            lax.dot_general(
+                jnp.concatenate([part, query_mark[n, m]], axis=1), keys, NT,
+                preferred_element_type=F32,
+            )
+            for n, part in enumerate((q_low, q_high))
+        ]
+        top = jnp.maximum(
+            jnp.max(both[0], axis=1, keepdims=True), jnp.max(both[1], axis=1, keepdims=True)
         )
-        gq = jnp.concatenate(
-            [
-                jnp.sum(jnp.where(col == row + base, mine_g, 0.0), axis=1, keepdims=True)
-                for base in (0, HALF)
-            ],
-            axis=0,
-        )
-        keys = rb[1, half]
-        s_low = lax.dot_general(q_low, keys, NT, preferred_element_type=F32)
-        s_high = lax.dot_general(q_high, keys, NT, preferred_element_type=F32)
-        s_low = jnp.where(gq == key_low, s_low, -jnp.inf)
-        s_high = jnp.where(gq == key_high, s_high, -jnp.inf)
-        top = jnp.maximum(
-            jnp.max(s_low, axis=1, keepdims=True), jnp.max(s_high, axis=1, keepdims=True)
-        )
-        return s_low, s_high, top
+        return both[0], both[1], top
 
     def weigh(s_low, s_high, top, half):
         p_low = jnp.exp2((s_low - top) * scale)
@@ -249,27 +261,20 @@
         mixed += jnp.dot(p_high.astype(BF), vd[half, 512:1024, :], preferred_element_type=F32)
         return total, mixed
 
-    key_low, key_high = key_groups(c)
     spread_values(c)
-
-    def first_half(n, carry):
-        s_low, s_high, top = scores(chunk(n), c, key_low, key_high)
+    for n in range(4):
+        s_low, s_high, top = scores(chunk(n), c)
         total, mixed = weigh(s_low, s_high, top, c)
         top_v[n] = top
         sum_v[n] = total
         acc[n] = mixed
-        return carry
-
-    lax.fori_loop(0, 4, first_half, 0)
-
-    for n in range(3):
-        drain(theirs[n], PR + n)
-    other_low, other_high = key_groups(1 - c)
+
+    drain(theirs[0], PR)
+    drain(theirs[1], PR + 1)
     spread_values(1 - c)
-
-    def second_half(n, carry):
+    for n in range(4):
         m = chunk(n)
-        s_low, s_high, top = scores(m, 1 - c, other_low, other_high)
+        s_low, s_high, top = scores(m, 1 - c)
         before = top_v[n]
         top = jnp.maximum(before, top)
         total, mixed = weigh(s_low, s_high, top, 1 - c)
@@ -284,9 +289,6 @@
                 cb.at[lax.div(x, 2), lax.div(head, 4), lax.rem(x, 2)],
                 CS, CR, turn_x(k), owner_y, 2 * m + c, owner_c, None if k else spare.at[1],
             )
-        return carry
-
-    lax.fori_loop(0, 4, second_half, 0)
 
     for i in (1, 3, 2):
         remote(wo.at[c, y], wo.at[c, lax.rem(y + i, 4)], OS + i, OR + i, along_y(4 - i)).wait_recv()
@@ -336,6 +338,8 @@
     pltpu.VMEM((1, 128), F32),
     pltpu.VMEM((3, 2, 512, 128), BF),
     pltpu.VMEM((2, 16, 1, 128), F32),
+    pltpu.VMEM((2, 512, 128), BF),
+    pltpu.VMEM((2, 4, 256, 128), BF),
     pltpu.VMEM((2, 1024, 128), BF),
     pltpu.VMEM((512, 128), BF),
     pltpu.VMEM((2, 4, 2, HALF, 128), BF),

time: 44.3 us -> 44.4 us (level)
  no operation moved by 1% of the time
where the time goes in v3:
time: 44.4 us; the launch traced here: 44.3 us
  Pallas kernels  42.7 us (96%)
  local copies, waits for them, and re-layouts  1.59 us (4%)
    pallas_call x1, Pallas kernels, shards(): pl.pallas_call(kernel, out_shape=jax.ShapeDtypeStruct((1, ROWS, D), BF),...  42.7 us
    unnamed x1, local copies, waits for them, and re-layouts  1.59 us

profile of v3, /device:TPU:95, one launch (start us, length us, event | category | flops | bytes accessed | tf_op | source)
XLA Modules:
  0.0 44.3 jit_solution(7542562505919328849)
XLA Ops:
  0.0 42.7 %attend.1 = bf16[1,64,1280]{2,1,0:T(8,128)(2,1)} custom-call(bf16[1,64,1280]{2,1,0:T(8,128)(2,1)} %frames.1, s32[1,64]{1,0:T(1,128)} %bitcast.1, s32[1,32]{1,0:T(1,128)} %plan.1, f32[1280]{0:T(1024)} %gain.1, bf16[1280,384]{1,0:T(8,128)(2,1)} %w_qkv.1, bf16[128,1280]{1,0:T(8,128)(2,1)} %w_out.1), custom_call_target="tpu_custom_call" | custom-call | tf_op jit(solution)/shard_map/attend/pallas_call | solution.py:359
  42.7 1.6 %copy.8 = bf16[1,64,1280]{2,1,0:T(8,128)(2,1)} copy(bf16[1,64,1280]{2,1,0:T(8,128)(2,1)} %attend.1) | data formatting | bytes 327680

commit v4 on v3

--- a/solution.py
+++ b/solution.py
@@ -15,16 +15,17 @@
 ROWS = 64
 HALF = 32
 FR, DE, PL, GA, WL, WOL = 0, 1, 2, 3, 4, 5
-XS, XR = 6, 10
-WS, WR = 14, 15
-OS, OR = 16, 20
-FS, FT = 24, 28
-SBS = 32
-QR = 33
-GS, GR = 36, 37
-PS, PR = 38, 41
-CS, CR = 44, 45
-NSEM = 46
+XS, XR = 6, 12
+WS, WR = 18, 19
+OS, OR = 20, 24
+QS, QV = 28, 32
+FS, FT = 36, 40
+SBS = 44
+QR = 45
+GS, GR = 48, 49
+PS, PR = 50, 53
+CS, CR = 56, 57
+NSEM = 58
 
 
 def halves(block):
@@ -34,7 +35,7 @@
 def kernel(
     frames, dest, plan, gain, w_qkv, w_out, out,
     raw, dest_v, plan_v, gain_v, xb, w, wo, sb, own_g, rb, gb, key_mark, query_mark, vd, co, cb, acc, top_v,
-    sum_v, spare, spare_g, sem, line_x, line_y,
+    sum_v, spare, spare_g, sem, line_x, line_y, line_z,
 ):
     g = lax.axis_index("grp")
     r = lax.axis_index("rep")
@@ -49,8 +50,14 @@
     def turn_x(i):
         return lax.rem(x + i, 4)
 
+    def along_x(i):
+        return at(turn_x(i), y, z, c)
+
     def along_y(i):
         return at(x, lax.rem(y + i, 4), z, c)
+
+    def along_z(i):
+        return at(x, y, lax.rem(z + i, 8), c)
 
     sibling = at(x, y, z, 1 - c)
 
@@ -96,7 +103,7 @@
     plane = [at(turn_x(i), y, z, c) for i in (1, 2, 3)]
     plane += [at(turn_x(i), y, z, 1 - c) for i in range(4)]
     partners = [along_y(i) for i in (1, 2, 3)] + plane
-    partners += [at(x, y, lax.rem(z + i, 8), c) for i in range(1, 8)]
+    partners += [along_z(i) for i in (1, 2, 6, 7)]
     for partner in partners:
         pl.semaphore_signal(barrier, inc=1, device_id=partner, device_id_type=MESH)
 
@@ -122,19 +129,28 @@
 
     pl.semaphore_wait(barrier, len(partners))
 
-    for i in (1, 3, 2):
-        remote(xb.at[0], xb.at[i], XS + i, XR + i, along_y(4 - i)).start()
+    upper, lower = pl.ds(0, HALF), pl.ds(HALF, HALF)
+
+    def row_copy(n):
+        block, to, part, source = (
+            (1, 3, upper, 0), (3, 1, lower, 0), (1, 3, lower, 0), (3, 1, upper, 0),
+            (2, 3, upper, 1), (2, 1, lower, 3),
+        )[n]
+        return remote(xb.at[source, part], xb.at[block, part], XS + n, XR + n, along_y(to))
+
+    for n in range(4):
+        row_copy(n).start()
     remote(w_qkv, w.at[c], WS, WR, sibling).start()
-    for partner in plane:
-        pl.semaphore_signal(line_x, inc=1, device_id=partner, device_id_type=MESH)
+    for i in (2, 6):
+        pl.semaphore_signal(line_z, inc=1, device_id=along_z(i), device_id_type=MESH)
 
     def project(i, s):
         part = jnp.dot(xb[i], w[s], preferred_element_type=F32)
         for p in range(3):
             two = part[:, 128 * p : 128 * p + 128]
-            upper, lower = two[:HALF], two[HALF:]
-            sb[i, 6 * s + 2 * p] = jnp.where(low, upper, halves(lower)).astype(BF)
-            sb[i, 6 * s + 2 * p + 1] = jnp.where(low, halves(upper), lower).astype(BF)
+            first, last = two[:HALF], two[HALF:]
+            sb[i, 6 * s + 2 * p] = jnp.where(low, first, halves(last)).astype(BF)
+            sb[i, 6 * s + 2 * p + 1] = jnp.where(low, halves(first), last).astype(BF)
 
     def scatter(i):
         tz = lax.rem(y + i, 4) + 4 * c
@@ -150,6 +166,12 @@
 
     loads[4].wait()
     project(0, c)
+    pl.semaphore_wait(line_z, 2)
+    for partner in plane:
+        pl.semaphore_signal(line_x, inc=1, device_id=partner, device_id_type=MESH)
+    for n in (0, 1):
+        row_copy(n).wait_recv()
+        row_copy(4 + n).start()
     pl.semaphore_wait(line_x, len(plane))
     for i in (1, 2, 3):
         pl.semaphore_signal(line_y, inc=1, device_id=along_y(i), device_id_type=MESH)
@@ -164,14 +186,28 @@
                 own_g, gb.at[cls, slot], GS, GR, turn_x(k), lax.rem(y + i, 4), y + 4 * c, cls,
                 None if k or i else spare_g,
             )
-    for i in (1, 3, 2):
-        remote(xb.at[0], xb.at[i], XS + i, XR + i, along_y(4 - i)).wait_recv()
+    for i, arrivals in ((1, (2,)), (3, (3,)), (2, (4, 5))):
+        for n in arrivals:
+            row_copy(n).wait_recv()
         project(i, 0)
         project(i, 1)
         scatter(i)
     loads[5].wait()
-    for i in (1, 3, 2):
-        remote(wo.at[c, y], wo.at[c, y], OS + i, OR + i, along_y(4 - i)).start()
+    opposite = lax.rem(y + 2, 4)
+
+    def quarter(ty, tx):
+        return wo.at[c, ty, pl.ds(pl.multiple_of(tx * HALF, HALF), HALF)]
+
+    def shard_copy(i):
+        ref = quarter(y, x) if i == 2 else wo.at[c, y]
+        return remote(ref, ref, OS + i, OR + i, along_y(4 - i))
+
+    def quarter_copy(i):
+        ref = quarter(opposite, x)
+        return remote(ref, ref, QS + i, QV + i, along_x(i))
+
+    for i in (2, 1, 3):
+        shard_copy(i).start()
 
     def to_sibling(i):
         ty = lax.rem(y + i, 4)
@@ -217,6 +253,9 @@
     drain(theirs[2], PR + 2)
     for m in range(4):
         mark_keys(1 - c, m)
+    shard_copy(2).wait_recv()
+    for i in (1, 2, 3):
+        quarter_copy(i).start()
     swap(0, QR + 1)
     swap(1, QR + 2)
     drain(rb.at[0, c], QR)
@@ -291,7 +330,11 @@
             )
 
     for i in (1, 3, 2):
-        remote(wo.at[c, y], wo.at[c, lax.rem(y + i, 4)], OS + i, OR + i, along_y(4 - i)).wait_recv()
+        if i == 2:
+            for k in (1, 2, 3):
+                quarter_copy(k).wait_recv()
+        else:
+            shard_copy(i).wait_recv()
         to_sibling(i).start()
 
     drain(cb, CR)
@@ -313,9 +356,11 @@
         weights = wo[:, :, :, cols].reshape(1024, 256)
         out[0, :, cols] = jnp.dot(context, weights, preferred_element_type=F32).astype(BF)
 
+    for n in range(6):
+        row_copy(n).wait_send()
     for i in (1, 2, 3):
-        remote(xb.at[0], xb.at[i], XS + i, XR + i, along_y(4 - i)).wait_send()
-        remote(wo.at[c, y], wo.at[c, y], OS + i, OR + i, along_y(4 - i)).wait_send()
+        shard_copy(i).wait_send()
+        quarter_copy(i).wait_send()
     remote(w_qkv, w.at[c], WS, WR, sibling).wait_send()
     for i in range(4):
         to_sibling(i).wait_send()
@@ -351,6 +396,7 @@
     pltpu.SemaphoreType.DMA((NSEM,)),
     pltpu.SemaphoreType.REGULAR,
     pltpu.SemaphoreType.REGULAR,
+    pltpu.SemaphoreType.REGULAR,
 ]
 
 

time: 44.4 us -> 42.9 us (0.966)
  the two profiles are of different devices: /device:TPU:95 before, /device:TPU:16 now
where the time goes in v4:
time: 42.9 us; the launch traced here: 42.8 us
  Pallas kernels  41.2 us (96%)
  local copies, waits for them, and re-layouts  1.59 us (4%)
    pallas_call x1, Pallas kernels, shards(): pl.pallas_call(kernel, out_shape=jax.ShapeDtypeStruct((1, ROWS, D), BF),...  41.2 us
    unnamed x1, local copies, waits for them, and re-layouts  1.59 us

profile of v4, /device:TPU:16, one launch (start us, length us, event | category | flops | bytes accessed | tf_op | source)
XLA Modules:
  0.0 42.8 jit_solution(17119171450213803588)
XLA Ops:
  0.0 41.2 %attend.1 = bf16[1,64,1280]{2,1,0:T(8,128)(2,1)} custom-call(bf16[1,64,1280]{2,1,0:T(8,128)(2,1)} %frames.1, s32[1,64]{1,0:T(1,128)} %bitcast.1, s32[1,32]{1,0:T(1,128)} %plan.1, f32[1280]{0:T(1024)} %gain.1, bf16[1280,384]{1,0:T(8,128)(2,1)} %w_qkv.1, bf16[128,1280]{1,0:T(8,128)(2,1)} %w_out.1), custom_call_target="tpu_custom_call" | custom-call | tf_op jit(solution)/shard_map/attend/pallas_call | solution.py:405
  41.2 1.6 %copy.8 = bf16[1,64,1280]{2,1,0:T(8,128)(2,1)} copy(bf16[1,64,1280]{2,1,0:T(8,128)(2,1)} %attend.1) | data formatting | bytes 327680

commit v5 on v4

--- a/solution.py
+++ b/solution.py
@@ -33,8 +33,8 @@
 
 
 def kernel(
-    frames, dest, plan, gain, w_qkv, w_out, out,
-    raw, dest_v, plan_v, gain_v, xb, w, wo, sb, own_g, rb, gb, key_mark, query_mark, vd, co, cb, acc, top_v,
+    frames, dest, plan, gain, w_qkv, w_out, out, wo,
+    raw, dest_v, plan_v, gain_v, xb, w, sb, own_g, rb, gb, key_mark, query_mark, vd, co, cb, acc, top_v,
     sum_v, spare, spare_g, sem, line_x, line_y, line_z,
 ):
     g = lax.axis_index("grp")
@@ -270,11 +270,8 @@
     owner_y, owner_c = lax.rem(z, 4), lax.div(z, 4)
     scale = 0.125 * math.log2(math.e)
 
-    def chunk(n):
-        return lax.rem(lax.div(z, 2) + 2 + n * 3, 4)
-
     def scores(m, half):
-        q = rb[0, c, pl.ds(pl.multiple_of(m * 128, 128), 128), :]
+        q = rb[0, c, 128 * m : 128 * m + 128, :]
         turned = halves(q)
         none = jnp.zeros_like(q)
         q_low = jnp.concatenate([jnp.where(low, q, none), jnp.where(low, turned, none)], axis=0)
@@ -300,34 +297,38 @@
         mixed += jnp.dot(p_high.astype(BF), vd[half, 512:1024, :], preferred_element_type=F32)
         return total, mixed
 
+    def first_part(m):
+        s_low, s_high, top = scores(m, c)
+        total, mixed = weigh(s_low, s_high, top, c)
+        top_v[m] = top
+        sum_v[m] = total
+        acc[m] = mixed
+
+    def second_part(m):
+        s_low, s_high, top = scores(m, 1 - c)
+        before = top_v[m]
+        top = jnp.maximum(before, top)
+        total, mixed = weigh(s_low, s_high, top, 1 - c)
+        factor = jnp.exp2((before - top) * scale)
+        context = (acc[m] * factor + mixed) / (sum_v[m] * factor + total)
+        co[128 * m : 128 * m + 128, :] = jnp.where(low, context[:128], context[128:]).astype(BF)
+        for k in (2, 1, 3, 0):
+            push(
+                co.at[pl.ds(128 * m + HALF * turn_x(k), HALF)],
+                cb.at[lax.div(x, 2), lax.div(head, 4), lax.rem(x, 2)],
+                CS, CR, turn_x(k), owner_y, 2 * m + c, owner_c, None if k else spare.at[1],
+            )
+
     spread_values(c)
-    for n in range(4):
-        s_low, s_high, top = scores(chunk(n), c)
-        total, mixed = weigh(s_low, s_high, top, c)
-        top_v[n] = top
-        sum_v[n] = total
-        acc[n] = mixed
-
+    for m in range(3):
+        first_part(m)
     drain(theirs[0], PR)
     drain(theirs[1], PR + 1)
     spread_values(1 - c)
-    for n in range(4):
-        m = chunk(n)
-        s_low, s_high, top = scores(m, 1 - c)
-        before = top_v[n]
-        top = jnp.maximum(before, top)
-        total, mixed = weigh(s_low, s_high, top, 1 - c)
-        factor = jnp.exp2((before - top) * scale)
-        context = (acc[n] * factor + mixed) / (sum_v[n] * factor + total)
-        co[pl.ds(pl.multiple_of(m * 128, 128), 128), :] = jnp.where(
-            low, context[:128], context[128:]
-        ).astype(BF)
-        for k in (2, 1, 3, 0):
-            push(
-                co.at[pl.ds(m * 128 + HALF * turn_x(k), HALF)],
-                cb.at[lax.div(x, 2), lax.div(head, 4), lax.rem(x, 2)],
-                CS, CR, turn_x(k), owner_y, 2 * m + c, owner_c, None if k else spare.at[1],
-            )
+    for m in range(3):
+        second_part(m)
+    first_part(3)
+    second_part(3)
 
     for i in (1, 3, 2):
         if i == 2:
@@ -338,23 +339,16 @@
         to_sibling(i).start()
 
     drain(cb, CR)
-    pieces = []
     for tc in range(2):
         for ty in range(4):
             even, odd = cb[tc, ty, 0], cb[tc, ty, 1]
-            pieces.append(
-                jnp.concatenate(
-                    [jnp.where(low, even, halves(odd)), jnp.where(low, halves(even), odd)], axis=0
-                )
+            both = jnp.concatenate(
+                [jnp.where(low, even, halves(odd)), jnp.where(low, halves(even), odd)], axis=0
             )
-    context = jnp.concatenate(pieces, axis=1)
+            out[:, 512 * tc + 128 * ty : 512 * tc + 128 * ty + 128] = both
     for i in range(4):
         ty = lax.rem(y + i, 4)
         remote(wo.at[c, ty], wo.at[1 - c, ty], FS + i, FT + i, sibling).wait_recv()
-    for n in range(5):
-        cols = slice(256 * n, 256 * n + 256)
-        weights = wo[:, :, :, cols].reshape(1024, 256)
-        out[0, :, cols] = jnp.dot(context, weights, preferred_element_type=F32).astype(BF)
 
     for n in range(6):
         row_copy(n).wait_send()
@@ -378,7 +372,6 @@
     pltpu.VMEM((D,), F32),
     pltpu.VMEM((4, ROWS, D), BF),
     pltpu.VMEM((2, D, 384), BF),
-    pltpu.VMEM((2, 4, 128, D), BF),
     pltpu.VMEM((4, 12, HALF, 128), BF),
     pltpu.VMEM((1, 128), F32),
     pltpu.VMEM((3, 2, 512, 128), BF),
@@ -402,17 +395,22 @@
 
 def shards(frames, destination, plan, norm_gain, w_qkv, w_out):
     any_space = pl.BlockSpec(memory_space=pl.ANY)
-    return pl.pallas_call(
+    context, weights = pl.pallas_call(
         kernel,
-        out_shape=jax.ShapeDtypeStruct((1, ROWS, D), BF),
+        out_shape=(
+            jax.ShapeDtypeStruct((ROWS, 1024), BF),
+            jax.ShapeDtypeStruct((2, 4, 128, D), BF),
+        ),
         in_specs=[any_space] * 6,
-        out_specs=pl.BlockSpec(memory_space=pltpu.VMEM),
+        out_specs=(pl.BlockSpec(memory_space=pltpu.VMEM), any_space),
         scratch_shapes=SCRATCH,
         compiler_params=pltpu.CompilerParams(
             collective_id=0, has_side_effects=True, vmem_limit_bytes=60 * 2**20
         ),
         name="attend",
     )(frames, destination.reshape(1, ROWS), plan, norm_gain, w_qkv, w_out)
+    projected = jnp.dot(context, weights.reshape(1024, D), preferred_element_type=F32)
+    return projected.astype(BF)[None]
 
 
 def solution(mesh):

time: 42.9 us -> 42 us (0.979)
  the two profiles are of different devices: /device:TPU:16 before, /device:TPU:1 now
where the time goes in v5:
time: 42 us; the launch traced here: 41.9 us
  Pallas kernels  38.8 us (92%)
  matrix products  3.06 us (7%)
    pallas_call x1, Pallas kernels, shards(): pl.pallas_call(kernel, out_shape=(jax.ShapeDtypeStruct((ROWS, 1024), BF),...  38.8 us
    dot_general x1, matrix products, shards(): jnp.dot(context, weights.reshape(1024, D), preferred_element_type=F32)  3.06 us

profile of v5, /device:TPU:1, one launch (start us, length us, event | category | flops | bytes accessed | tf_op | source)
XLA Modules:
  0.0 41.9 jit_solution(15880077132637599445)
XLA Ops:
  0.0 38.8 %attend.1 = (bf16[64,1024]{1,0:T(8,128)(2,1)}, bf16[2,4,128,1280]{3,2,1,0:T(8,128)(2,1)}) custom-call(bf16[1,64,1280]{2,1,0:T(8,128)(2,1)} %frames.1, s32[1,64]{1,0:T(1,128)} %bitcast.7, s32[1,32]{1,0:T(1,128)} %plan.1, f32[1280]{0:T(1024)} %gain.1, bf16[1280,384]{1,0:T(8,128)(2,1)} %w_qkv.1, bf16[128,1280]{1,0:T(8,128)(2,1)} %w_out.1), custom_call_target="tpu_custom_call" | custom-call | tf_op jit(solution)/shard_map/attend/pallas_call | solution.py:398
  38.8 3.1 %fusion = bf16[1,64,1280]{2,1,0:T(8,128)(2,1)} fusion(bf16[64,1024]{1,0:T(8,128)(2,1)} %get-tuple-element.7, bf16[1024,1280]{1,0:T(8,128)(2,1)} %bitcast.6), kind=kOutput, calls=%fused_computation.1 | convolution fusion | flops 167854080 | bytes 2916352 | tf_op jit(solution)/shard_map/dot_general | solution.py:412

commit v6 on v5

--- a/solution.py
+++ b/solution.py
@@ -33,8 +33,8 @@
 
 
 def kernel(
-    frames, dest, plan, gain, w_qkv, w_out, out, wo,
-    raw, dest_v, plan_v, gain_v, xb, w, sb, own_g, rb, gb, key_mark, query_mark, vd, co, cb, acc, top_v,
+    frames, dest, plan, gain, w_qkv, w_out, out,
+    raw, dest_v, plan_v, gain_v, xb, w, wo, sb, own_g, rb, gb, key_mark, query_mark, vd, co, cb, acc, top_v,
     sum_v, spare, spare_g, sem, line_x, line_y, line_z,
 ):
     g = lax.axis_index("grp")
@@ -339,16 +339,23 @@
         to_sibling(i).start()
 
     drain(cb, CR)
+    pieces = []
     for tc in range(2):
         for ty in range(4):
             even, odd = cb[tc, ty, 0], cb[tc, ty, 1]
-            both = jnp.concatenate(
-                [jnp.where(low, even, halves(odd)), jnp.where(low, halves(even), odd)], axis=0
+            pieces.append(
+                jnp.concatenate(
+                    [jnp.where(low, even, halves(odd)), jnp.where(low, halves(even), odd)], axis=0
+                )
             )
-            out[:, 512 * tc + 128 * ty : 512 * tc + 128 * ty + 128] = both
+    context = jnp.concatenate(pieces, axis=1)
     for i in range(4):
         ty = lax.rem(y + i, 4)
         remote(wo.at[c, ty], wo.at[1 - c, ty], FS + i, FT + i, sibling).wait_recv()
+    for n in range(5):
+        cols = slice(256 * n, 256 * n + 256)
+        weights = wo[:, :, :, cols].reshape(1024, 256)
+        out[0, :, cols] = jnp.dot(context, weights, preferred_element_type=F32).astype(BF)
 
     for n in range(6):
         row_copy(n).wait_send()
@@ -372,6 +379,7 @@
     pltpu.VMEM((D,), F32),
     pltpu.VMEM((4, ROWS, D), BF),
     pltpu.VMEM((2, D, 384), BF),
+    pltpu.VMEM((2, 4, 128, D), BF),
     pltpu.VMEM((4, 12, HALF, 128), BF),
     pltpu.VMEM((1, 128), F32),
     pltpu.VMEM((3, 2, 512, 128), BF),
@@ -395,22 +403,17 @@
 
 def shards(frames, destination, plan, norm_gain, w_qkv, w_out):
     any_space = pl.BlockSpec(memory_space=pl.ANY)
-    context, weights = pl.pallas_call(
+    return pl.pallas_call(
         kernel,
-        out_shape=(
-            jax.ShapeDtypeStruct((ROWS, 1024), BF),
-            jax.ShapeDtypeStruct((2, 4, 128, D), BF),
-        ),
+        out_shape=jax.ShapeDtypeStruct((1, ROWS, D), BF),
         in_specs=[any_space] * 6,
-        out_specs=(pl.BlockSpec(memory_space=pltpu.VMEM), any_space),
+        out_specs=pl.BlockSpec(memory_space=pltpu.VMEM),
         scratch_shapes=SCRATCH,
         compiler_params=pltpu.CompilerParams(
             collective_id=0, has_side_effects=True, vmem_limit_bytes=60 * 2**20
         ),
         name="attend",
     )(frames, destination.reshape(1, ROWS), plan, norm_gain, w_qkv, w_out)
-    projected = jnp.dot(context, weights.reshape(1024, D), preferred_element_type=F32)
-    return projected.astype(BF)[None]
 
 
 def solution(mesh):

time: 42 us -> 41.3 us (0.983)
  matrix products: 3.06 us -> 0 us
  local copies, waits for them, and re-layouts: 0 us -> 1.59 us
  Pallas kernels: 38.8 us -> 39.6 us
    dot_general x1 -> x0, matrix products: 3.06 us -> none  [shards(): jnp.dot(context, weights.reshape(1024, D), preferred_element_type=F32)]
    unnamed x0 -> x1, local copies, waits for them, and re-layouts: none -> 1.59 us
    pallas_call x1, Pallas kernels: 38.8 us -> 39.6 us  [shards(): pl.pallas_call(kernel, out_shape=jax.ShapeDtypeStruct((1, ROWS, D), BF),...]
where the time goes in v6:
time: 41.3 us; the launch traced here: 41.2 us
  Pallas kernels  39.6 us (96%)
  local copies, waits for them, and re-layouts  1.59 us (4%)
    pallas_call x1, Pallas kernels, shards(): pl.pallas_call(kernel, out_shape=jax.ShapeDtypeStruct((1, ROWS, D), BF),...  39.6 us
    unnamed x1, local copies, waits for them, and re-layouts  1.59 us

profile of v6, /device:TPU:1, one launch (start us, length us, event | category | flops | bytes accessed | tf_op | source)
XLA Modules:
  0.0 41.2 jit_solution(13042064530532061037)
XLA Ops:
  0.0 39.6 %attend.1 = bf16[1,64,1280]{2,1,0:T(8,128)(2,1)} custom-call(bf16[1,64,1280]{2,1,0:T(8,128)(2,1)} %frames.1, s32[1,64]{1,0:T(1,128)} %bitcast.1, s32[1,32]{1,0:T(1,128)} %plan.1, f32[1280]{0:T(1024)} %gain.1, bf16[1280,384]{1,0:T(8,128)(2,1)} %w_qkv.1, bf16[128,1280]{1,0:T(8,128)(2,1)} %w_out.1), custom_call_target="tpu_custom_call" | custom-call | tf_op jit(solution)/shard_map/attend/pallas_call | solution.py:406
  39.6 1.6 %copy.8 = bf16[1,64,1280]{2,1,0:T(8,128)(2,1)} copy(bf16[1,64,1280]{2,1,0:T(8,128)(2,1)} %attend.1) | data formatting | bytes 327680

commit v7 on v6

--- a/solution.py
+++ b/solution.py
@@ -25,7 +25,8 @@
 GS, GR = 48, 49
 PS, PR = 50, 53
 CS, CR = 56, 57
-NSEM = 58
+RS = 58
+NSEM = 63
 
 
 def halves(block):
@@ -35,7 +36,7 @@
 def kernel(
     frames, dest, plan, gain, w_qkv, w_out, out,
     raw, dest_v, plan_v, gain_v, xb, w, wo, sb, own_g, rb, gb, key_mark, query_mark, vd, co, cb, acc, top_v,
-    sum_v, spare, spare_g, sem, line_x, line_y, line_z,
+    sum_v, spare, spare_g, result, sem, line_x, line_y, line_z,
 ):
     g = lax.axis_index("grp")
     r = lax.axis_index("rep")
@@ -108,6 +109,31 @@
         pl.semaphore_signal(barrier, inc=1, device_id=partner, device_id_type=MESH)
 
     low = lax.broadcasted_iota(jnp.int32, (1, 128), 1) < 64
+    loads[0].wait()
+    loads[3].wait()
+    values = raw[...].astype(F32)
+    mean = jnp.mean(values, axis=1, keepdims=True)
+    centered = values - mean
+    variance = jnp.mean(centered * centered, axis=1, keepdims=True)
+    xb[0] = (centered * lax.rsqrt(variance + 1e-05) * gain_v[...][None, :]).astype(BF)
+
+    pl.semaphore_wait(barrier, len(partners))
+
+    upper, lower = pl.ds(0, HALF), pl.ds(HALF, HALF)
+
+    def row_copy(n):
+        block, to, part, source = (
+            (1, 3, upper, 0), (3, 1, lower, 0), (1, 3, lower, 0), (3, 1, upper, 0),
+            (2, 3, upper, 1), (2, 1, lower, 3),
+        )[n]
+        return remote(xb.at[source, part], xb.at[block, part], XS + n, XR + n, along_y(to))
+
+    for i in (2, 6):
+        pl.semaphore_signal(line_z, inc=1, device_id=along_z(i), device_id_type=MESH)
+    for n in range(4):
+        row_copy(n).start()
+    remote(w_qkv, w.at[c], WS, WR, sibling).start()
+
     loads[1].wait()
     loads[2].wait()
     row32 = lax.broadcasted_iota(jnp.int32, (32, 32), 0)
@@ -119,31 +145,6 @@
     group = jnp.sum(jnp.where(hot, plan_rows, 0.0), axis=0, keepdims=True)
     own_g[...] = jnp.concatenate([group, group], axis=1)
 
-    loads[0].wait()
-    loads[3].wait()
-    values = raw[...].astype(F32)
-    mean = jnp.mean(values, axis=1, keepdims=True)
-    centered = values - mean
-    variance = jnp.mean(centered * centered, axis=1, keepdims=True)
-    xb[0] = (centered * lax.rsqrt(variance + 1e-05) * gain_v[...][None, :]).astype(BF)
-
-    pl.semaphore_wait(barrier, len(partners))
-
-    upper, lower = pl.ds(0, HALF), pl.ds(HALF, HALF)
-
-    def row_copy(n):
-        block, to, part, source = (
-            (1, 3, upper, 0), (3, 1, lower, 0), (1, 3, lower, 0), (3, 1, upper, 0),
-            (2, 3, upper, 1), (2, 1, lower, 3),
-        )[n]
-        return remote(xb.at[source, part], xb.at[block, part], XS + n, XR + n, along_y(to))
-
-    for n in range(4):
-        row_copy(n).start()
-    remote(w_qkv, w.at[c], WS, WR, sibling).start()
-    for i in (2, 6):
-        pl.semaphore_signal(line_z, inc=1, device_id=along_z(i), device_id_type=MESH)
-
     def project(i, s):
         part = jnp.dot(xb[i], w[s], preferred_element_type=F32)
         for p in range(3):
@@ -152,9 +153,9 @@
             sb[i, 6 * s + 2 * p] = jnp.where(low, first, halves(last)).astype(BF)
             sb[i, 6 * s + 2 * p + 1] = jnp.where(low, halves(first), last).astype(BF)
 
-    def scatter(i):
+    def scatter(i, blocks):
         tz = lax.rem(y + i, 4) + 4 * c
-        for s in range(3):
+        for s in blocks:
             sub = 3 * y + s
             kind, block = lax.div(sub, 4), lax.rem(sub, 4)
             ty = block + 1 - 2 * lax.rem(block, 2)
@@ -169,17 +170,17 @@
     pl.semaphore_wait(line_z, 2)
     for partner in plane:
         pl.semaphore_signal(line_x, inc=1, device_id=partner, device_id_type=MESH)
+    pl.semaphore_wait(line_x, len(plane))
+    for i in (1, 2, 3):
+        pl.semaphore_signal(line_y, inc=1, device_id=along_y(i), device_id_type=MESH)
     for n in (0, 1):
         row_copy(n).wait_recv()
         row_copy(4 + n).start()
-    pl.semaphore_wait(line_x, len(plane))
-    for i in (1, 2, 3):
-        pl.semaphore_signal(line_y, inc=1, device_id=along_y(i), device_id_type=MESH)
     remote(w_qkv, w.at[1 - c], WS, WR, sibling).wait_recv()
     project(0, 1 - c)
+    scatter(0, (1,))
     pl.semaphore_wait(line_y, 3)
-
-    scatter(0)
+    scatter(0, (0, 2))
     for k in (2, 1, 3, 0):
         for i in (2, 1, 3, 0):
             push(
@@ -191,7 +192,7 @@
             row_copy(n).wait_recv()
         project(i, 0)
         project(i, 1)
-        scatter(i)
+        scatter(i, (0, 2, 1))
     loads[5].wait()
     opposite = lax.rem(y + 2, 4)
 
@@ -253,12 +254,12 @@
     drain(theirs[2], PR + 2)
     for m in range(4):
         mark_keys(1 - c, m)
+    swap(0, QR + 1)
+    swap(1, QR + 2)
+    drain(rb.at[0, c], QR)
     shard_copy(2).wait_recv()
     for i in (1, 2, 3):
         quarter_copy(i).start()
-    swap(0, QR + 1)
-    swap(1, QR + 2)
-    drain(rb.at[0, c], QR)
 
     def spread_values(half):
         vals = rb[2, half]
@@ -338,6 +339,17 @@
             shard_copy(i).wait_recv()
         to_sibling(i).start()
 
+    for n in range(6):
+        row_copy(n).wait_send()
+    for i in (1, 2, 3):
+        shard_copy(i).wait_send()
+        quarter_copy(i).wait_send()
+    remote(w_qkv, w.at[c], WS, WR, sibling).wait_send()
+    drain(sb, SBS)
+    for n in range(3):
+        remote(mine[n], mine[n], PS + n, PR + n, sibling).wait_send()
+    drain(gb.at[c], GS)
+
     drain(cb, CR)
     pieces = []
     for tc in range(2):
@@ -352,24 +364,20 @@
     for i in range(4):
         ty = lax.rem(y + i, 4)
         remote(wo.at[c, ty], wo.at[1 - c, ty], FS + i, FT + i, sibling).wait_recv()
+    leaving = []
     for n in range(5):
         cols = slice(256 * n, 256 * n + 256)
         weights = wo[:, :, :, cols].reshape(1024, 256)
-        out[0, :, cols] = jnp.dot(context, weights, preferred_element_type=F32).astype(BF)
-
-    for n in range(6):
-        row_copy(n).wait_send()
-    for i in (1, 2, 3):
-        shard_copy(i).wait_send()
-        quarter_copy(i).wait_send()
-    remote(w_qkv, w.at[c], WS, WR, sibling).wait_send()
+        result[:, cols] = jnp.dot(context, weights, preferred_element_type=F32).astype(BF)
+        piece = local(result.at[:, cols], out.at[0, :, cols], RS + n)
+        piece.start()
+        leaving.append(piece)
+
     for i in range(4):
         to_sibling(i).wait_send()
-    drain(sb, SBS)
-    for n in range(3):
-        remote(mine[n], mine[n], PS + n, PR + n, sibling).wait_send()
-    drain(gb.at[c], GS)
     drain(co, CS)
+    for piece in leaving:
+        piece.wait()
 
 
 SCRATCH = [
@@ -394,6 +402,7 @@
     pltpu.VMEM((4, 256, 1), F32),
     pltpu.VMEM((2, HALF, 128), BF),
     pltpu.VMEM((1, 128), F32),
+    pltpu.VMEM((ROWS, D), BF),
     pltpu.SemaphoreType.DMA((NSEM,)),
     pltpu.SemaphoreType.REGULAR,
     pltpu.SemaphoreType.REGULAR,
@@ -407,7 +416,7 @@
         kernel,
         out_shape=jax.ShapeDtypeStruct((1, ROWS, D), BF),
         in_specs=[any_space] * 6,
-        out_specs=pl.BlockSpec(memory_space=pltpu.VMEM),
+        out_specs=any_space,
         scratch_shapes=SCRATCH,
         compiler_params=pltpu.CompilerParams(
             collective_id=0, has_side_effects=True, vmem_limit_bytes=60 * 2**20

time: 41.3 us -> 40.8 us (0.988)
  Pallas kernels: 39.6 us -> 39.1 us
    pallas_call x1, Pallas kernels: 39.6 us -> 39.1 us  [shards(): pl.pallas_call(kernel, out_shape=jax.ShapeDtypeStruct((1, ROWS, D), BF),...]
where the time goes in v7:
time: 40.8 us; the launch traced here: 40.7 us
  Pallas kernels  39.1 us (96%)
  local copies, waits for them, and re-layouts  1.59 us (4%)
    pallas_call x1, Pallas kernels, shards(): pl.pallas_call(kernel, out_shape=jax.ShapeDtypeStruct((1, ROWS, D), BF),...  39.1 us
    unnamed x1, local copies, waits for them, and re-layouts  1.59 us

profile of v7, /device:TPU:1, one launch (start us, length us, event | category | flops | bytes accessed | tf_op | source)
XLA Modules:
  0.0 40.7 jit_solution(17021042925439729533)
XLA Ops:
  0.0 39.1 %attend.1 = bf16[1,64,1280]{2,1,0:T(8,128)(2,1)} custom-call(bf16[1,64,1280]{2,1,0:T(8,128)(2,1)} %frames.1, s32[1,64]{1,0:T(1,128)} %bitcast.1, s32[1,32]{1,0:T(1,128)} %plan.1, f32[1280]{0:T(1024)} %gain.1, bf16[1280,384]{1,0:T(8,128)(2,1)} %w_qkv.1, bf16[128,1280]{1,0:T(8,128)(2,1)} %w_out.1), custom_call_target="tpu_custom_call" | custom-call | tf_op jit(solution)/shard_map/attend/pallas_call | solution.py:415
  39.1 1.6 %copy.8 = bf16[1,64,1280]{2,1,0:T(8,128)(2,1)} copy(bf16[1,64,1280]{2,1,0:T(8,128)(2,1)} %attend.1) | data formatting | bytes 327680

commit v8 on v7

--- a/solution.py
+++ b/solution.py
@@ -25,8 +25,8 @@
 GS, GR = 48, 49
 PS, PR = 50, 53
 CS, CR = 56, 57
-RS = 58
-NSEM = 63
+RS = 59
+NSEM = 64
 
 
 def halves(block):
@@ -36,7 +36,7 @@
 def kernel(
     frames, dest, plan, gain, w_qkv, w_out, out,
     raw, dest_v, plan_v, gain_v, xb, w, wo, sb, own_g, rb, gb, key_mark, query_mark, vd, co, cb, acc, top_v,
-    sum_v, spare, spare_g, result, sem, line_x, line_y, line_z,
+    sum_v, spare, spare_g, near, result, sem, line_x, line_y, line_z,
 ):
     g = lax.axis_index("grp")
     r = lax.axis_index("rep")
@@ -154,7 +154,7 @@
             sb[i, 6 * s + 2 * p + 1] = jnp.where(low, halves(first), last).astype(BF)
 
     def scatter(i, blocks):
-        tz = lax.rem(y + i, 4) + 4 * c
+        tz = lax.rem(y + i, 4) + 4 * (1 - c)
         for s in blocks:
             sub = 3 * y + s
             kind, block = lax.div(sub, 4), lax.rem(sub, 4)
@@ -184,7 +184,7 @@
     for k in (2, 1, 3, 0):
         for i in (2, 1, 3, 0):
             push(
-                own_g, gb.at[cls, slot], GS, GR, turn_x(k), lax.rem(y + i, 4), y + 4 * c, cls,
+                own_g, gb.at[cls, slot], GS, GR, turn_x(k), lax.rem(y + i, 4), y + 4 * (1 - c), cls,
                 None if k or i else spare_g,
             )
     for i, arrivals in ((1, (2,)), (3, (3,)), (2, (4, 5))):
@@ -267,8 +267,9 @@
         vd[half, 0:512, :] = jnp.where(low, vals, turned)
         vd[half, 512:1024, :] = jnp.where(low, turned, vals)
 
-    head = (y + 1 - 2 * lax.rem(y, 2)) * 4 + x
-    owner_y, owner_c = lax.rem(z, 4), lax.div(z, 4)
+    owner_y, owner_c = lax.rem(z, 4), 1 - lax.div(z, 4)
+    away = lax.rem(y + 4 - owner_y, 4)
+    place = away + lax.div(away, 2) * (5 - 2 * away)
     scale = 0.125 * math.log2(math.e)
 
     def scores(m, half):
@@ -316,8 +317,8 @@
         for k in (2, 1, 3, 0):
             push(
                 co.at[pl.ds(128 * m + HALF * turn_x(k), HALF)],
-                cb.at[lax.div(x, 2), lax.div(head, 4), lax.rem(x, 2)],
-                CS, CR, turn_x(k), owner_y, 2 * m + c, owner_c, None if k else spare.at[1],
+                cb.at[place, lax.div(x, 2), lax.rem(x, 2)],
+                CS, CR + lax.div(place, 3), turn_x(k), owner_y, 2 * m + c, owner_c, None if k else spare.at[1],
             )
 
     spread_values(c)
@@ -350,25 +351,36 @@
         remote(mine[n], mine[n], PS + n, PR + n, sibling).wait_send()
     drain(gb.at[c], GS)
 
-    drain(cb, CR)
-    pieces = []
-    for tc in range(2):
-        for ty in range(4):
-            even, odd = cb[tc, ty, 0], cb[tc, ty, 1]
-            pieces.append(
+    def gathered(p):
+        both = []
+        for tc in range(2):
+            even, odd = cb[p, tc, 0], cb[p, tc, 1]
+            both.append(
                 jnp.concatenate(
                     [jnp.where(low, even, halves(odd)), jnp.where(low, halves(even), odd)], axis=0
                 )
             )
-    context = jnp.concatenate(pieces, axis=1)
+        return jnp.concatenate(both, axis=1)
+
+    def product(p, context, cols):
+        ty = lax.rem(y + (0, 1, 3, 2)[p], 4)
+        ty = ty + 1 - 2 * lax.rem(ty, 2)
+        weights = wo[:, ty, :, cols].reshape(256, 256)
+        return jnp.dot(context, weights, preferred_element_type=F32)
+
+    drain(cb.at[pl.ds(0, 3)], CR)
     for i in range(4):
         ty = lax.rem(y + i, 4)
         remote(wo.at[c, ty], wo.at[1 - c, ty], FS + i, FT + i, sibling).wait_recv()
+    contexts = [gathered(p) for p in range(3)]
+    spans = [slice(256 * n, 256 * n + 256) for n in range(5)]
+    for cols in spans:
+        near[:, cols] = sum(product(p, contexts[p], cols) for p in range(3))
+    drain(cb.at[3], CR + 1)
+    context = gathered(3)
     leaving = []
-    for n in range(5):
-        cols = slice(256 * n, 256 * n + 256)
-        weights = wo[:, :, :, cols].reshape(1024, 256)
-        result[:, cols] = jnp.dot(context, weights, preferred_element_type=F32).astype(BF)
+    for n, cols in enumerate(spans):
+        result[:, cols] = (near[:, cols] + product(3, context, cols)).astype(BF)
         piece = local(result.at[:, cols], out.at[0, :, cols], RS + n)
         piece.start()
         leaving.append(piece)
@@ -396,12 +408,13 @@
     pltpu.VMEM((2, 4, 256, 128), BF),
     pltpu.VMEM((2, 1024, 128), BF),
     pltpu.VMEM((512, 128), BF),
-    pltpu.VMEM((2, 4, 2, HALF, 128), BF),
+    pltpu.VMEM((4, 2, 2, HALF, 128), BF),
     pltpu.VMEM((4, 256, 128), F32),
     pltpu.VMEM((4, 256, 1), F32),
     pltpu.VMEM((4, 256, 1), F32),
     pltpu.VMEM((2, HALF, 128), BF),
     pltpu.VMEM((1, 128), F32),
+    pltpu.VMEM((ROWS, D), F32),
     pltpu.VMEM((ROWS, D), BF),
     pltpu.SemaphoreType.DMA((NSEM,)),
     pltpu.SemaphoreType.REGULAR,

time: 40.8 us -> 39.5 us (0.968)
  the two profiles are of different devices: /device:TPU:1 before, /device:TPU:64 now
where the time goes in v8:
time: 39.5 us; the launch traced here: 39.4 us
  Pallas kernels  37.8 us (96%)
  local copies, waits for them, and re-layouts  1.59 us (4%)
    pallas_call x1, Pallas kernels, shards(): pl.pallas_call(kernel, out_shape=jax.ShapeDtypeStruct((1, ROWS, D), BF),...  37.8 us
    unnamed x1, local copies, waits for them, and re-layouts  1.59 us

profile of v8, /device:TPU:64, one launch (start us, length us, event | category | flops | bytes accessed | tf_op | source)
XLA Modules:
  0.0 39.4 jit_solution(3398738241820256143)
XLA Ops:
  0.0 37.8 %attend.1 = bf16[1,64,1280]{2,1,0:T(8,128)(2,1)} custom-call(bf16[1,64,1280]{2,1,0:T(8,128)(2,1)} %frames.1, s32[1,64]{1,0:T(1,128)} %bitcast.1, s32[1,32]{1,0:T(1,128)} %plan.1, f32[1280]{0:T(1024)} %gain.1, bf16[1280,384]{1,0:T(8,128)(2,1)} %w_qkv.1, bf16[128,1280]{1,0:T(8,128)(2,1)} %w_out.1), custom_call_target="tpu_custom_call" | custom-call | tf_op jit(solution)/shard_map/attend/pallas_call | solution.py:428
  37.8 1.6 %copy.8 = bf16[1,64,1280]{2,1,0:T(8,128)(2,1)} copy(bf16[1,64,1280]{2,1,0:T(8,128)(2,1)} %attend.1) | data formatting | bytes 327680

commit v9 on v8

--- a/solution.py
+++ b/solution.py
@@ -26,7 +26,8 @@
 PS, PR = 50, 53
 CS, CR = 56, 57
 RS = 59
-NSEM = 64
+GF = 64
+NSEM = 68
 
 
 def halves(block):
@@ -123,8 +124,8 @@
 
     def row_copy(n):
         block, to, part, source = (
-            (1, 3, upper, 0), (3, 1, lower, 0), (1, 3, lower, 0), (3, 1, upper, 0),
-            (2, 3, upper, 1), (2, 1, lower, 3),
+            (1, 3, upper, 0), (2, 1, lower, 0), (1, 3, lower, 0), (2, 1, upper, 0),
+            (3, 3, upper, 1), (3, 1, lower, 2),
         )[n]
         return remote(xb.at[source, part], xb.at[block, part], XS + n, XR + n, along_y(to))
 
@@ -145,16 +146,21 @@
     group = jnp.sum(jnp.where(hot, plan_rows, 0.0), axis=0, keepdims=True)
     own_g[...] = jnp.concatenate([group, group], axis=1)
 
-    def project(i, s):
-        part = jnp.dot(xb[i], w[s], preferred_element_type=F32)
-        for p in range(3):
-            two = part[:, 128 * p : 128 * p + 128]
-            first, last = two[:HALF], two[HALF:]
-            sb[i, 6 * s + 2 * p] = jnp.where(low, first, halves(last)).astype(BF)
-            sb[i, 6 * s + 2 * p + 1] = jnp.where(low, halves(first), last).astype(BF)
+    along = (0, 1, 3, 2)
+
+    def project(start, count, s):
+        rows = xb[start : start + count].reshape(count * ROWS, D)
+        part = jnp.dot(rows, w[s], preferred_element_type=F32)
+        for n in range(count):
+            for p in range(3):
+                two = part[n * ROWS : (n + 1) * ROWS, 128 * p : 128 * p + 128]
+                first, last = two[:HALF], two[HALF:]
+                spot = 6 * s + 2 * p
+                sb[start + n, spot] = jnp.where(low, first, halves(last)).astype(BF)
+                sb[start + n, spot + 1] = jnp.where(low, halves(first), last).astype(BF)
 
     def scatter(i, blocks):
-        tz = lax.rem(y + i, 4) + 4 * (1 - c)
+        tz = lax.rem(y + along[i], 4) + 4 * (1 - c)
         for s in blocks:
             sub = 3 * y + s
             kind, block = lax.div(sub, 4), lax.rem(sub, 4)
@@ -166,7 +172,7 @@
                 )
 
     loads[4].wait()
-    project(0, c)
+    project(0, 1, c)
     pl.semaphore_wait(line_z, 2)
     for partner in plane:
         pl.semaphore_signal(line_x, inc=1, device_id=partner, device_id_type=MESH)
@@ -177,22 +183,26 @@
         row_copy(n).wait_recv()
         row_copy(4 + n).start()
     remote(w_qkv, w.at[1 - c], WS, WR, sibling).wait_recv()
-    project(0, 1 - c)
+    project(0, 1, 1 - c)
     scatter(0, (1,))
     pl.semaphore_wait(line_y, 3)
     scatter(0, (0, 2))
     for k in (2, 1, 3, 0):
-        for i in (2, 1, 3, 0):
-            push(
-                own_g, gb.at[cls, slot], GS, GR, turn_x(k), lax.rem(y + i, 4), y + 4 * (1 - c), cls,
-                None if k or i else spare_g,
-            )
-    for i, arrivals in ((1, (2,)), (3, (3,)), (2, (4, 5))):
-        for n in arrivals:
-            row_copy(n).wait_recv()
-        project(i, 0)
-        project(i, 1)
-        scatter(i, (0, 2, 1))
+        push(
+            own_g, gb.at[cls, slot], GS, GR, turn_x(k), y, y + 4 * (1 - c), cls,
+            None if k else spare_g,
+        )
+    for n in (2, 3):
+        row_copy(n).wait_recv()
+    for s in range(2):
+        project(1, 2, s)
+    scatter(1, (0, 2, 1))
+    scatter(2, (0, 2, 1))
+    for n in (4, 5):
+        row_copy(n).wait_recv()
+    for s in range(2):
+        project(3, 1, s)
+    scatter(3, (0, 2, 1))
     loads[5].wait()
     opposite = lax.rem(y + 2, 4)
 
@@ -248,7 +258,18 @@
         query_mark[0, m] = jnp.where(lane < 32, miss, 0.0).astype(BF)
         query_mark[1, m] = jnp.where((lane >= 32) & (lane < 64), miss, 0.0).astype(BF)
 
-    swap(2, GR)
+    owner_y, owner_c = lax.rem(z, 4), 1 - lax.div(z, 4)
+    drain(gb.at[c], GR)
+
+    def pass_groups(i):
+        return remote(gb.at[c], gb.at[c], GF + i, GR, along_y(i))
+
+    @pl.when(y == owner_y)
+    def _():
+        for i in (2, 1, 3):
+            pass_groups(i).start()
+
+    remote(gb.at[c], gb.at[c], PS + 2, PR + 2, sibling).start()
     for m in range(4):
         mark_keys(c, m)
     drain(theirs[2], PR + 2)
@@ -267,7 +288,6 @@
         vd[half, 0:512, :] = jnp.where(low, vals, turned)
         vd[half, 512:1024, :] = jnp.where(low, turned, vals)
 
-    owner_y, owner_c = lax.rem(z, 4), 1 - lax.div(z, 4)
     away = lax.rem(y + 4 - owner_y, 4)
     place = away + lax.div(away, 2) * (5 - 2 * away)
     scale = 0.125 * math.log2(math.e)
@@ -349,7 +369,13 @@
     drain(sb, SBS)
     for n in range(3):
         remote(mine[n], mine[n], PS + n, PR + n, sibling).wait_send()
-    drain(gb.at[c], GS)
+    drain(gb.at[c, pl.ds(0, 4)], GS)
+
+    @pl.when(y == owner_y)
+    def _():
+        for i in (1, 2, 3):
+            pass_groups(i).wait_send()
+
 
     def gathered(p):
         both = []

time: 39.5 us -> 44.1 us (1.12)
  the two profiles are of different devices: /device:TPU:64 before, /device:TPU:1 now
where the time goes in v9:
time: 44.1 us; the launch traced here: 44 us
  Pallas kernels  42.4 us (96%)
  local copies, waits for them, and re-layouts  1.59 us (4%)
    pallas_call x1, Pallas kernels, shards(): pl.pallas_call(kernel, out_shape=jax.ShapeDtypeStruct((1, ROWS, D), BF),...  42.4 us
    unnamed x1, local copies, waits for them, and re-layouts  1.59 us

profile of v9, /device:TPU:1, one launch (start us, length us, event | category | flops | bytes accessed | tf_op | source)
XLA Modules:
  0.0 44.0 jit_solution(6633520654672608806)
XLA Ops:
  0.0 42.4 %attend.1 = bf16[1,64,1280]{2,1,0:T(8,128)(2,1)} custom-call(bf16[1,64,1280]{2,1,0:T(8,128)(2,1)} %frames.1, s32[1,64]{1,0:T(1,128)} %bitcast.1, s32[1,32]{1,0:T(1,128)} %plan.1, f32[1280]{0:T(1024)} %gain.1, bf16[1280,384]{1,0:T(8,128)(2,1)} %w_qkv.1, bf16[128,1280]{1,0:T(8,128)(2,1)} %w_out.1), custom_call_target="tpu_custom_call" | custom-call | tf_op jit(solution)/shard_map/attend/pallas_call | solution.py:454
  42.4 1.6 %copy.8 = bf16[1,64,1280]{2,1,0:T(8,128)(2,1)} copy(bf16[1,64,1280]{2,1,0:T(8,128)(2,1)} %attend.1) | data formatting | bytes 327680

commit v10 on v9

--- a/solution.py
+++ b/solution.py
@@ -26,8 +26,7 @@
 PS, PR = 50, 53
 CS, CR = 56, 57
 RS = 59
-GF = 64
-NSEM = 68
+NSEM = 64
 
 
 def halves(block):
@@ -187,11 +186,6 @@
     scatter(0, (1,))
     pl.semaphore_wait(line_y, 3)
     scatter(0, (0, 2))
-    for k in (2, 1, 3, 0):
-        push(
-            own_g, gb.at[cls, slot], GS, GR, turn_x(k), y, y + 4 * (1 - c), cls,
-            None if k else spare_g,
-        )
     for n in (2, 3):
         row_copy(n).wait_recv()
     for s in range(2):
@@ -203,6 +197,12 @@
     for s in range(2):
         project(3, 1, s)
     scatter(3, (0, 2, 1))
+    for k in (2, 1, 3, 0):
+        for i in (2, 1, 3, 0):
+            push(
+                own_g, gb.at[cls, slot], GS, GR, turn_x(k), lax.rem(y + i, 4), y + 4 * (1 - c),
+                cls, None if k or i else spare_g,
+            )
     loads[5].wait()
     opposite = lax.rem(y + 2, 4)
 
@@ -258,18 +258,7 @@
         query_mark[0, m] = jnp.where(lane < 32, miss, 0.0).astype(BF)
         query_mark[1, m] = jnp.where((lane >= 32) & (lane < 64), miss, 0.0).astype(BF)
 
-    owner_y, owner_c = lax.rem(z, 4), 1 - lax.div(z, 4)
-    drain(gb.at[c], GR)
-
-    def pass_groups(i):
-        return remote(gb.at[c], gb.at[c], GF + i, GR, along_y(i))
-
-    @pl.when(y == owner_y)
-    def _():
-        for i in (2, 1, 3):
-            pass_groups(i).start()
-
-    remote(gb.at[c], gb.at[c], PS + 2, PR + 2, sibling).start()
+    swap(2, GR)
     for m in range(4):
         mark_keys(c, m)
     drain(theirs[2], PR + 2)
@@ -288,6 +277,7 @@
         vd[half, 0:512, :] = jnp.where(low, vals, turned)
         vd[half, 512:1024, :] = jnp.where(low, turned, vals)
 
+    owner_y, owner_c = lax.rem(z, 4), 1 - lax.div(z, 4)
     away = lax.rem(y + 4 - owner_y, 4)
     place = away + lax.div(away, 2) * (5 - 2 * away)
     scale = 0.125 * math.log2(math.e)
@@ -369,13 +359,7 @@
     drain(sb, SBS)
     for n in range(3):
         remote(mine[n], mine[n], PS + n, PR + n, sibling).wait_send()
-    drain(gb.at[c, pl.ds(0, 4)], GS)
-
-    @pl.when(y == owner_y)
-    def _():
-        for i in (1, 2, 3):
-            pass_groups(i).wait_send()
-
+    drain(gb.at[c], GS)
 
     def gathered(p):
         both = []

time: 44.1 us -> 41.5 us (0.941)
  Pallas kernels: 42.4 us -> 39.5 us
    pallas_call x1, Pallas kernels: 42.4 us -> 39.5 us  [shards(): pl.pallas_call(kernel, out_shape=jax.ShapeDtypeStruct((1, ROWS, D), BF),...]
where the time goes in v10:
time: 41.5 us; the launch traced here: 41.1 us
  Pallas kernels  39.5 us (95%)
  local copies, waits for them, and re-layouts  1.59 us (4%)
    pallas_call x1, Pallas kernels, shards(): pl.pallas_call(kernel, out_shape=jax.ShapeDtypeStruct((1, ROWS, D), BF),...  39.5 us
    unnamed x1, local copies, waits for them, and re-layouts  1.59 us

profile of v10, /device:TPU:1, one launch (start us, length us, event | category | flops | bytes accessed | tf_op | source)
XLA Modules:
  0.0 41.1 jit_solution(15959321556666264324)
XLA Ops:
  0.0 39.5 %attend.1 = bf16[1,64,1280]{2,1,0:T(8,128)(2,1)} custom-call(bf16[1,64,1280]{2,1,0:T(8,128)(2,1)} %frames.1, s32[1,64]{1,0:T(1,128)} %bitcast.1, s32[1,32]{1,0:T(1,128)} %plan.1, f32[1280]{0:T(1024)} %gain.1, bf16[1280,384]{1,0:T(8,128)(2,1)} %w_qkv.1, bf16[128,1280]{1,0:T(8,128)(2,1)} %w_out.1), custom_call_target="tpu_custom_call" | custom-call | tf_op jit(solution)/shard_map/attend/pallas_call | solution.py:438
  39.6 1.6 %copy.8 = bf16[1,64,1280]{2,1,0:T(8,128)(2,1)} copy(bf16[1,64,1280]{2,1,0:T(8,128)(2,1)} %attend.1) | data formatting | bytes 327680

commit v11 on v10

--- a/solution.py
+++ b/solution.py
@@ -26,7 +26,8 @@
 PS, PR = 50, 53
 CS, CR = 56, 57
 RS = 59
-NSEM = 64
+GX, GY = 64, 68
+NSEM = 72
 
 
 def halves(block):
@@ -35,15 +36,15 @@
 
 def kernel(
     frames, dest, plan, gain, w_qkv, w_out, out,
-    raw, dest_v, plan_v, gain_v, xb, w, wo, sb, own_g, rb, gb, key_mark, query_mark, vd, co, cb, acc, top_v,
-    sum_v, spare, spare_g, near, result, sem, line_x, line_y, line_z,
+    raw, dest_v, plan_v, gain_v, xb, w, wo, sb, line_g, rb, gb, key_mark, query_mark, vd, co, cb, acc, top_v,
+    sum_v, near, result, sem, line_x, line_y, line_z,
 ):
     g = lax.axis_index("grp")
     r = lax.axis_index("rep")
     x, z = lax.div(g, 8), lax.rem(g, 8)
     y, c = lax.div(r, 2), lax.rem(r, 2)
-    cls = lax.rem(z, 2)
-    slot = lax.div(z, 2) * 4 + x
+    cls = lax.div(z, 4)
+    slot = lax.rem(z, 4) * 4 + x
 
     def at(tx, ty, tz, tc):
         return (tx * 8 + tz, ty * 2 + tc)
@@ -71,20 +72,8 @@
     def local(src, dst, s):
         return pltpu.make_async_copy(src, dst, sem.at[s])
 
-    def push(src, dst, ssem, rsem, tx, ty, tz, tc, dummy):
-        if dummy is None:
-            remote(src, dst, ssem, rsem, at(tx, ty, tz, tc)).start()
-            return
-        same = (ty == y) & (tz == z) & (tc == c)
-
-        @pl.when(jnp.logical_not(same))
-        def _():
-            remote(src, dst, ssem, rsem, at(tx, ty, tz, tc)).start()
-
-        @pl.when(same)
-        def _():
-            local(src, dst, rsem).start()
-            local(src, dummy, ssem).start()
+    def push(src, dst, ssem, rsem, tx, ty, tz, tc):
+        remote(src, dst, ssem, rsem, at(tx, ty, tz, tc)).start()
 
     def drain(ref, s):
         local(ref, ref, s).wait()
@@ -143,7 +132,13 @@
     )
     hot = dest_v[...] == lax.broadcasted_iota(jnp.int32, (32, ROWS), 0)
     group = jnp.sum(jnp.where(hot, plan_rows, 0.0), axis=0, keepdims=True)
-    own_g[...] = jnp.concatenate([group, group], axis=1)
+    line_g[0] = jnp.concatenate([group, group], axis=1)
+
+    def group_copy(i):
+        return remote(line_g.at[0], line_g.at[i], GX + i, GY + i, along_y(4 - i))
+
+    for i in (2, 1, 3):
+        group_copy(i).start()
 
     along = (0, 1, 3, 2)
 
@@ -167,7 +162,7 @@
             for k in (2, 1, 3, 0):
                 push(
                     sb.at[i, 4 * s + turn_x(k)], rb.at[kind, cls, pl.ds(slot * HALF, HALF)],
-                    SBS, QR + kind, turn_x(k), ty, tz, cls, None if k else spare.at[0],
+                    SBS, QR + kind, turn_x(k), ty, tz, cls,
                 )
 
     loads[4].wait()
@@ -181,6 +176,12 @@
     for n in (0, 1):
         row_copy(n).wait_recv()
         row_copy(4 + n).start()
+    for i in (0, 1, 3, 2):
+        if i:
+            group_copy(i).wait_recv()
+        tz = lax.rem(y + i, 4) + 4 * (1 - c)
+        for k in (2, 1, 3, 0):
+            push(line_g.at[i], gb.at[cls, slot], GS, GR, turn_x(k), y, tz, cls)
     remote(w_qkv, w.at[1 - c], WS, WR, sibling).wait_recv()
     project(0, 1, 1 - c)
     scatter(0, (1,))
@@ -197,12 +198,6 @@
     for s in range(2):
         project(3, 1, s)
     scatter(3, (0, 2, 1))
-    for k in (2, 1, 3, 0):
-        for i in (2, 1, 3, 0):
-            push(
-                own_g, gb.at[cls, slot], GS, GR, turn_x(k), lax.rem(y + i, 4), y + 4 * (1 - c),
-                cls, None if k or i else spare_g,
-            )
     loads[5].wait()
     opposite = lax.rem(y + 2, 4)
 
@@ -328,7 +323,7 @@
             push(
                 co.at[pl.ds(128 * m + HALF * turn_x(k), HALF)],
                 cb.at[place, lax.div(x, 2), lax.rem(x, 2)],
-                CS, CR + lax.div(place, 3), turn_x(k), owner_y, 2 * m + c, owner_c, None if k else spare.at[1],
+                CS, CR + lax.div(place, 3), turn_x(k), owner_y, 4 * c + m, owner_c,
             )
 
     spread_values(c)
@@ -360,6 +355,8 @@
     for n in range(3):
         remote(mine[n], mine[n], PS + n, PR + n, sibling).wait_send()
     drain(gb.at[c], GS)
+    for i in (1, 2, 3):
+        group_copy(i).wait_send()
 
     def gathered(p):
         both = []
@@ -411,7 +408,7 @@
     pltpu.VMEM((2, D, 384), BF),
     pltpu.VMEM((2, 4, 128, D), BF),
     pltpu.VMEM((4, 12, HALF, 128), BF),
-    pltpu.VMEM((1, 128), F32),
+    pltpu.VMEM((4, 1, 128), F32),
     pltpu.VMEM((3, 2, 512, 128), BF),
     pltpu.VMEM((2, 16, 1, 128), F32),
     pltpu.VMEM((2, 512, 128), BF),
@@ -422,8 +419,6 @@
     pltpu.VMEM((4, 256, 128), F32),
     pltpu.VMEM((4, 256, 1), F32),
     pltpu.VMEM((4, 256, 1), F32),
-    pltpu.VMEM((2, HALF, 128), BF),
-    pltpu.VMEM((1, 128), F32),
     pltpu.VMEM((ROWS, D), F32),
     pltpu.VMEM((ROWS, D), BF),
     pltpu.SemaphoreType.DMA((NSEM,)),

time: 41.5 us -> 40.7 us (0.981)
  the two profiles are of different devices: /device:TPU:1 before, /device:TPU:80 now
where the time goes in v11:
time: 40.7 us; the launch traced here: 40.6 us
  Pallas kernels  39 us (96%)
  local copies, waits for them, and re-layouts  1.59 us (4%)
    pallas_call x1, Pallas kernels, shards(): pl.pallas_call(kernel, out_shape=jax.ShapeDtypeStruct((1, ROWS, D), BF),...  39 us
    unnamed x1, local copies, waits for them, and re-layouts  1.59 us

profile of v11, /device:TPU:80, one launch (start us, length us, event | category | flops | bytes accessed | tf_op | source)
XLA Modules:
  0.0 40.6 jit_solution(12201971459307356623)
XLA Ops:
  0.0 39.0 %attend.1 = bf16[1,64,1280]{2,1,0:T(8,128)(2,1)} custom-call(bf16[1,64,1280]{2,1,0:T(8,128)(2,1)} %frames.1, s32[1,64]{1,0:T(1,128)} %bitcast.1, s32[1,32]{1,0:T(1,128)} %plan.1, f32[1280]{0:T(1024)} %gain.1, bf16[1280,384]{1,0:T(8,128)(2,1)} %w_qkv.1, bf16[128,1280]{1,0:T(8,128)(2,1)} %w_out.1), custom_call_target="tpu_custom_call" | custom-call | tf_op jit(solution)/shard_map/attend/pallas_call | solution.py:433
  39.0 1.6 %copy.8 = bf16[1,64,1280]{2,1,0:T(8,128)(2,1)} copy(bf16[1,64,1280]{2,1,0:T(8,128)(2,1)} %attend.1) | data formatting | bytes 327680

commit v12 on v11

--- a/solution.py
+++ b/solution.py
@@ -43,8 +43,8 @@
     r = lax.axis_index("rep")
     x, z = lax.div(g, 8), lax.rem(g, 8)
     y, c = lax.div(r, 2), lax.rem(r, 2)
-    cls = lax.div(z, 4)
-    slot = lax.rem(z, 4) * 4 + x
+    cls = lax.rem(z, 2)
+    slot = lax.div(z, 2) * 4 + x
 
     def at(tx, ty, tz, tc):
         return (tx * 8 + tz, ty * 2 + tc)
@@ -74,6 +74,9 @@
 
     def push(src, dst, ssem, rsem, tx, ty, tz, tc):
         remote(src, dst, ssem, rsem, at(tx, ty, tz, tc)).start()
+
+    def plane_of(i):
+        return lax.rem(2 * lax.rem(y + i, 4) + 5 * (1 - c), 8)
 
     def drain(ref, s):
         local(ref, ref, s).wait()
@@ -154,7 +157,7 @@
                 sb[start + n, spot + 1] = jnp.where(low, halves(first), last).astype(BF)
 
     def scatter(i, blocks):
-        tz = lax.rem(y + along[i], 4) + 4 * (1 - c)
+        tz = plane_of(along[i])
         for s in blocks:
             sub = 3 * y + s
             kind, block = lax.div(sub, 4), lax.rem(sub, 4)
@@ -179,7 +182,7 @@
     for i in (0, 1, 3, 2):
         if i:
             group_copy(i).wait_recv()
-        tz = lax.rem(y + i, 4) + 4 * (1 - c)
+        tz = plane_of(i)
         for k in (2, 1, 3, 0):
             push(line_g.at[i], gb.at[cls, slot], GS, GR, turn_x(k), y, tz, cls)
     remote(w_qkv, w.at[1 - c], WS, WR, sibling).wait_recv()
@@ -272,7 +275,7 @@
         vd[half, 0:512, :] = jnp.where(low, vals, turned)
         vd[half, 512:1024, :] = jnp.where(low, turned, vals)
 
-    owner_y, owner_c = lax.rem(z, 4), 1 - lax.div(z, 4)
+    owner_y, owner_c = lax.div(lax.rem(z + 3 * lax.rem(z, 2), 8), 2), 1 - lax.rem(z, 2)
     away = lax.rem(y + 4 - owner_y, 4)
     place = away + lax.div(away, 2) * (5 - 2 * away)
     scale = 0.125 * math.log2(math.e)
@@ -323,7 +326,7 @@
             push(
                 co.at[pl.ds(128 * m + HALF * turn_x(k), HALF)],
                 cb.at[place, lax.div(x, 2), lax.rem(x, 2)],
-                CS, CR + lax.div(place, 3), turn_x(k), owner_y, 4 * c + m, owner_c,
+                CS, CR + lax.div(place, 3), turn_x(k), owner_y, 2 * m + c, owner_c,
             )
 
     spread_values(c)

time: 40.7 us -> 40.6 us (level)
  the two profiles are of different devices: /device:TPU:80 before, /device:TPU:1 now
where the time goes in v12:
time: 40.6 us; the launch traced here: 40.5 us
  Pallas kernels  38.9 us (96%)
  local copies, waits for them, and re-layouts  1.59 us (4%)
    pallas_call x1, Pallas kernels, shards(): pl.pallas_call(kernel, out_shape=jax.ShapeDtypeStruct((1, ROWS, D), BF),...  38.9 us
    unnamed x1, local copies, waits for them, and re-layouts  1.59 us

profile of v12, /device:TPU:1, one launch (start us, length us, event | category | flops | bytes accessed | tf_op | source)
XLA Modules:
  0.0 40.5 jit_solution(11638904250591596183)
XLA Ops:
  0.0 38.9 %attend.1 = bf16[1,64,1280]{2,1,0:T(8,128)(2,1)} custom-call(bf16[1,64,1280]{2,1,0:T(8,128)(2,1)} %frames.1, s32[1,64]{1,0:T(1,128)} %bitcast.1, s32[1,32]{1,0:T(1,128)} %plan.1, f32[1280]{0:T(1024)} %gain.1, bf16[1280,384]{1,0:T(8,128)(2,1)} %w_qkv.1, bf16[128,1280]{1,0:T(8,128)(2,1)} %w_out.1), custom_call_target="tpu_custom_call" | custom-call | tf_op jit(solution)/shard_map/attend/pallas_call | solution.py:436
  38.9 1.6 %copy.8 = bf16[1,64,1280]{2,1,0:T(8,128)(2,1)} copy(bf16[1,64,1280]{2,1,0:T(8,128)(2,1)} %attend.1) | data formatting | bytes 327680

commit v13 on v12

--- a/solution.py
+++ b/solution.py
@@ -76,7 +76,7 @@
         remote(src, dst, ssem, rsem, at(tx, ty, tz, tc)).start()
 
     def plane_of(i):
-        return lax.rem(2 * lax.rem(y + i, 4) + 5 * (1 - c), 8)
+        return lax.rem(2 * lax.rem(y + i, 4) + 1 + 5 * c, 8)
 
     def drain(ref, s):
         local(ref, ref, s).wait()
@@ -275,7 +275,8 @@
         vd[half, 0:512, :] = jnp.where(low, vals, turned)
         vd[half, 512:1024, :] = jnp.where(low, turned, vals)
 
-    owner_y, owner_c = lax.div(lax.rem(z + 3 * lax.rem(z, 2), 8), 2), 1 - lax.rem(z, 2)
+    owner_c = 1 - lax.rem(z, 2)
+    owner_y = lax.div(lax.rem(z + 2 * owner_c, 8), 2)
     away = lax.rem(y + 4 - owner_y, 4)
     place = away + lax.div(away, 2) * (5 - 2 * away)
     scale = 0.125 * math.log2(math.e)

time: 40.6 us -> 40.2 us (level)
  no operation moved by 1% of the time
where the time goes in v13:
time: 40.2 us; the launch traced here: 40.1 us
  Pallas kernels  38.5 us (96%)
  local copies, waits for them, and re-layouts  1.59 us (4%)
    pallas_call x1, Pallas kernels, shards(): pl.pallas_call(kernel, out_shape=jax.ShapeDtypeStruct((1, ROWS, D), BF),...  38.5 us
    unnamed x1, local copies, waits for them, and re-layouts  1.59 us

profile of v13, /device:TPU:1, one launch (start us, length us, event | category | flops | bytes accessed | tf_op | source)
XLA Modules:
  0.0 40.1 jit_solution(1742043337018684599)
XLA Ops:
  0.0 38.5 %attend.1 = bf16[1,64,1280]{2,1,0:T(8,128)(2,1)} custom-call(bf16[1,64,1280]{2,1,0:T(8,128)(2,1)} %frames.1, s32[1,64]{1,0:T(1,128)} %bitcast.1, s32[1,32]{1,0:T(1,128)} %plan.1, f32[1280]{0:T(1024)} %gain.1, bf16[1280,384]{1,0:T(8,128)(2,1)} %w_qkv.1, bf16[128,1280]{1,0:T(8,128)(2,1)} %w_out.1), custom_call_target="tpu_custom_call" | custom-call | tf_op jit(solution)/shard_map/attend/pallas_call | solution.py:437
  38.5 1.6 %copy.8 = bf16[1,64,1280]{2,1,0:T(8,128)(2,1)} copy(bf16[1,64,1280]{2,1,0:T(8,128)(2,1)} %attend.1) | data formatting | bytes 327680

commit v14 on v13

--- a/solution.py
+++ b/solution.py
@@ -265,9 +265,6 @@
     swap(0, QR + 1)
     swap(1, QR + 2)
     drain(rb.at[0, c], QR)
-    shard_copy(2).wait_recv()
-    for i in (1, 2, 3):
-        quarter_copy(i).start()
 
     def spread_values(half):
         vals = rb[2, half]
@@ -331,15 +328,17 @@
             )
 
     spread_values(c)
-    for m in range(3):
+    for m in range(4):
         first_part(m)
     drain(theirs[0], PR)
     drain(theirs[1], PR + 1)
     spread_values(1 - c)
-    for m in range(3):
+    for m in range(4):
         second_part(m)
-    first_part(3)
-    second_part(3)
+        if m == 1:
+            shard_copy(2).wait_recv()
+            for i in (1, 2, 3):
+                quarter_copy(i).start()
 
     for i in (1, 3, 2):
         if i == 2:

time: 40.2 us -> 42.5 us (1.057)
  the two profiles are of different devices: /device:TPU:1 before, /device:TPU:33 now
where the time goes in v14:
time: 42.5 us; the launch traced here: 42.4 us
  Pallas kernels  40.8 us (96%)
  local copies, waits for them, and re-layouts  1.59 us (4%)
    pallas_call x1, Pallas kernels, shards(): pl.pallas_call(kernel, out_shape=jax.ShapeDtypeStruct((1, ROWS, D), BF),...  40.8 us
    unnamed x1, local copies, waits for them, and re-layouts  1.59 us

profile of v14, /device:TPU:33, one launch (start us, length us, event | category | flops | bytes accessed | tf_op | source)
XLA Modules:
  0.0 42.4 jit_solution(15245668114825773431)
XLA Ops:
  0.0 40.8 %attend.1 = bf16[1,64,1280]{2,1,0:T(8,128)(2,1)} custom-call(bf16[1,64,1280]{2,1,0:T(8,128)(2,1)} %frames.1, s32[1,64]{1,0:T(1,128)} %bitcast.1, s32[1,32]{1,0:T(1,128)} %plan.1, f32[1280]{0:T(1024)} %gain.1, bf16[1280,384]{1,0:T(8,128)(2,1)} %w_qkv.1, bf16[128,1280]{1,0:T(8,128)(2,1)} %w_out.1), custom_call_target="tpu_custom_call" | custom-call | tf_op jit(solution)/shard_map/attend/pallas_call | solution.py:436
  40.8 1.6 %copy.8 = bf16[1,64,1280]{2,1,0:T(8,128)(2,1)} copy(bf16[1,64,1280]{2,1,0:T(8,128)(2,1)} %attend.1) | data formatting | bytes 327680

commit v15 on v13

--- a/solution.py
+++ b/solution.py
@@ -187,43 +187,42 @@
             push(line_g.at[i], gb.at[cls, slot], GS, GR, turn_x(k), y, tz, cls)
     remote(w_qkv, w.at[1 - c], WS, WR, sibling).wait_recv()
     project(0, 1, 1 - c)
+    opposite = lax.rem(y + 2, 4)
+
+    def quarter(ty, tx):
+        return wo.at[c, ty, pl.ds(pl.multiple_of(tx * HALF, HALF), HALF)]
+
+    def shard_copy(i):
+        ref = quarter(y, x) if i == 2 else wo.at[c, y]
+        return remote(ref, ref, OS + i, OR + i, along_y(4 - i))
+
+    def quarter_copy(i):
+        ref = quarter(opposite, x)
+        return remote(ref, ref, QS + i, QV + i, along_x(i))
+
+    def to_sibling(i):
+        ty = lax.rem(y + i, 4)
+        return remote(wo.at[c, ty], wo.at[c, ty], FS + i, FT + i, sibling)
+
     scatter(0, (1,))
     pl.semaphore_wait(line_y, 3)
     scatter(0, (0, 2))
+    loads[5].wait()
+    shard_copy(2).start()
     for n in (2, 3):
         row_copy(n).wait_recv()
     for s in range(2):
         project(1, 2, s)
     scatter(1, (0, 2, 1))
     scatter(2, (0, 2, 1))
+    for i in (1, 3):
+        shard_copy(i).start()
+    to_sibling(0).start()
     for n in (4, 5):
         row_copy(n).wait_recv()
     for s in range(2):
         project(3, 1, s)
     scatter(3, (0, 2, 1))
-    loads[5].wait()
-    opposite = lax.rem(y + 2, 4)
-
-    def quarter(ty, tx):
-        return wo.at[c, ty, pl.ds(pl.multiple_of(tx * HALF, HALF), HALF)]
-
-    def shard_copy(i):
-        ref = quarter(y, x) if i == 2 else wo.at[c, y]
-        return remote(ref, ref, OS + i, OR + i, along_y(4 - i))
-
-    def quarter_copy(i):
-        ref = quarter(opposite, x)
-        return remote(ref, ref, QS + i, QV + i, along_x(i))
-
-    for i in (2, 1, 3):
-        shard_copy(i).start()
-
-    def to_sibling(i):
-        ty = lax.rem(y + i, 4)
-        return remote(wo.at[c, ty], wo.at[c, ty], FS + i, FT + i, sibling)
-
-    to_sibling(0).start()
-
     mine = [rb.at[1, c], rb.at[2, c], gb.at[c]]
     theirs = [rb.at[1, 1 - c], rb.at[2, 1 - c], gb.at[1 - c]]
 
@@ -262,12 +261,12 @@
     drain(theirs[2], PR + 2)
     for m in range(4):
         mark_keys(1 - c, m)
+    shard_copy(2).wait_recv()
+    for i in (1, 2, 3):
+        quarter_copy(i).start()
     swap(0, QR + 1)
     swap(1, QR + 2)
     drain(rb.at[0, c], QR)
-    shard_copy(2).wait_recv()
-    for i in (1, 2, 3):
-        quarter_copy(i).start()
 
     def spread_values(half):
         vals = rb[2, half]
@@ -338,16 +337,14 @@
     spread_values(1 - c)
     for m in range(3):
         second_part(m)
-    first_part(3)
-    second_part(3)
-
-    for i in (1, 3, 2):
-        if i == 2:
+        if m == 2:
             for k in (1, 2, 3):
                 quarter_copy(k).wait_recv()
         else:
-            shard_copy(i).wait_recv()
-        to_sibling(i).start()
+            shard_copy((1, 3)[m]).wait_recv()
+        to_sibling((1, 3, 2)[m]).start()
+    first_part(3)
+    second_part(3)
 
     for n in range(6):
         row_copy(n).wait_send()

time: 40.2 us -> 40.3 us (level)
  no operation moved by 1% of the time
where the time goes in v15:
time: 40.3 us; the launch traced here: 40.2 us
  Pallas kernels  38.6 us (96%)
  local copies, waits for them, and re-layouts  1.59 us (4%)
    pallas_call x1, Pallas kernels, shards(): pl.pallas_call(kernel, out_shape=jax.ShapeDtypeStruct((1, ROWS, D), BF),...  38.6 us
    unnamed x1, local copies, waits for them, and re-layouts  1.59 us

profile of v15, /device:TPU:1, one launch (start us, length us, event | category | flops | bytes accessed | tf_op | source)
XLA Modules:
  0.0 40.2 jit_solution(13495570100916439688)
XLA Ops:
  0.0 38.6 %attend.1 = bf16[1,64,1280]{2,1,0:T(8,128)(2,1)} custom-call(bf16[1,64,1280]{2,1,0:T(8,128)(2,1)} %frames.1, s32[1,64]{1,0:T(1,128)} %bitcast.1, s32[1,32]{1,0:T(1,128)} %plan.1, f32[1280]{0:T(1024)} %gain.1, bf16[1280,384]{1,0:T(8,128)(2,1)} %w_qkv.1, bf16[128,1280]{1,0:T(8,128)(2,1)} %w_out.1), custom_call_target="tpu_custom_call" | custom-call | tf_op jit(solution)/shard_map/attend/pallas_call | solution.py:434
  38.6 1.6 %copy.8 = bf16[1,64,1280]{2,1,0:T(8,128)(2,1)} copy(bf16[1,64,1280]{2,1,0:T(8,128)(2,1)} %attend.1) | data formatting | bytes 327680

commit v16 on v15

--- a/solution.py
+++ b/solution.py
@@ -25,7 +25,6 @@
 GS, GR = 48, 49
 PS, PR = 50, 53
 CS, CR = 56, 57
-RS = 59
 GX, GY = 64, 68
 NSEM = 72
 
@@ -37,7 +36,7 @@
 def kernel(
     frames, dest, plan, gain, w_qkv, w_out, out,
     raw, dest_v, plan_v, gain_v, xb, w, wo, sb, line_g, rb, gb, key_mark, query_mark, vd, co, cb, acc, top_v,
-    sum_v, near, result, sem, line_x, line_y, line_z,
+    sum_v, near, sem, line_x, line_y, line_z,
 ):
     g = lax.axis_index("grp")
     r = lax.axis_index("rep")
@@ -215,14 +214,15 @@
         project(1, 2, s)
     scatter(1, (0, 2, 1))
     scatter(2, (0, 2, 1))
-    for i in (1, 3):
-        shard_copy(i).start()
-    to_sibling(0).start()
     for n in (4, 5):
         row_copy(n).wait_recv()
     for s in range(2):
         project(3, 1, s)
     scatter(3, (0, 2, 1))
+    for i in (1, 3):
+        shard_copy(i).start()
+    to_sibling(0).start()
+
     mine = [rb.at[1, c], rb.at[2, c], gb.at[c]]
     theirs = [rb.at[1, 1 - c], rb.at[2, 1 - c], gb.at[1 - c]]
 
@@ -337,14 +337,16 @@
     spread_values(1 - c)
     for m in range(3):
         second_part(m)
-        if m == 2:
+        if m == 0:
             for k in (1, 2, 3):
                 quarter_copy(k).wait_recv()
-        else:
-            shard_copy((1, 3)[m]).wait_recv()
-        to_sibling((1, 3, 2)[m]).start()
+            to_sibling(2).start()
     first_part(3)
     second_part(3)
+
+    for i in (1, 3):
+        shard_copy(i).wait_recv()
+        to_sibling(i).start()
 
     for n in range(6):
         row_copy(n).wait_send()
@@ -386,18 +388,12 @@
         near[:, cols] = sum(product(p, contexts[p], cols) for p in range(3))
     drain(cb.at[3], CR + 1)
     context = gathered(3)
-    leaving = []
-    for n, cols in enumerate(spans):
-        result[:, cols] = (near[:, cols] + product(3, context, cols)).astype(BF)
-        piece = local(result.at[:, cols], out.at[0, :, cols], RS + n)
-        piece.start()
-        leaving.append(piece)
+    for cols in spans:
+        out[0, :, cols] = (near[:, cols] + product(3, context, cols)).astype(BF)
 
     for i in range(4):
         to_sibling(i).wait_send()
     drain(co, CS)
-    for piece in leaving:
-        piece.wait()
 
 
 SCRATCH = [
@@ -421,7 +417,6 @@
     pltpu.VMEM((4, 256, 1), F32),
     pltpu.VMEM((4, 256, 1), F32),
     pltpu.VMEM((ROWS, D), F32),
-    pltpu.VMEM((ROWS, D), BF),
     pltpu.SemaphoreType.DMA((NSEM,)),
     pltpu.SemaphoreType.REGULAR,
     pltpu.SemaphoreType.REGULAR,
@@ -435,10 +430,10 @@
         kernel,
         out_shape=jax.ShapeDtypeStruct((1, ROWS, D), BF),
         in_specs=[any_space] * 6,
-        out_specs=any_space,
+        out_specs=pl.BlockSpec(memory_space=pltpu.VMEM),
         scratch_shapes=SCRATCH,
         compiler_params=pltpu.CompilerParams(
-            collective_id=0, has_side_effects=True, vmem_limit_bytes=60 * 2**20
+            collective_id=0, has_side_effects=True, vmem_limit_bytes=55008 * 2**10
         ),
         name="attend",
     )(frames, destination.reshape(1, ROWS), plan, norm_gain, w_qkv, w_out)

time: 40.3 us -> 40.1 us (level)
  Pallas kernels: 38.6 us -> 37.9 us
  local copies, waits for them, and re-layouts: 1.59 us -> 2.03 us
    pallas_call x1, Pallas kernels: 38.6 us -> 37.9 us  [shards(): pl.pallas_call(kernel, out_shape=jax.ShapeDtypeStruct((1, ROWS, D), BF),...]
    unnamed x1 -> x7, local copies, waits for them, and re-layouts: 1.59 us -> 2.03 us
where the time goes in v16:
time: 40.1 us; the launch traced here: 40 us
  Pallas kernels  37.9 us (95%)
  local copies, waits for them, and re-layouts  2.03 us (5%)
    pallas_call x1, Pallas kernels, shards(): pl.pallas_call(kernel, out_shape=jax.ShapeDtypeStruct((1, ROWS, D), BF),...  37.9 us
    unnamed x7, local copies, waits for them, and re-layouts  2.03 us

profile of v16, /device:TPU:1, one launch (start us, length us, event | category | flops | bytes accessed | tf_op | source)
XLA Modules:
  0.0 40.0 jit_solution(14917972738420385761)
XLA Ops:
  0.0 0.0 copy-start.2
  0.0 0.0 copy-start.1
  0.0 0.7 %copy-done.2 = s32[1,32]{1,0:T(1,128)S(1)} copy-done((s32[1,32]{1,0:T(1,128)S(1)}, s32[1,32]{1,0:T(1,128)}, u32[]{:S(2)}) %copy-start.2) | copy-done | bytes 152
  0.7 0.0 copy-done.1
  0.7 0.0 copy-start
  0.7 0.7 %copy-done = f32[1280]{0:T(1024)S(1)} copy-done((f32[1280]{0:T(1024)S(1)}, f32[1280]{0:T(1024)}, u32[]{:S(2)}) %copy-start) | copy-done | bytes 5144
  1.4 37.9 %attend.1 = bf16[1,64,1280]{2,1,0:T(8,128)(2,1)S(1)} custom-call(bf16[1,64,1280]{2,1,0:T(8,128)(2,1)} %frames.1, s32[1,64]{1,0:T(1,128)S(1)} %bitcast.1, s32[1,32]{1,0:T(1,128)S(1)} %copy-done.2, f32[1280]{0:T(1024)S(1)} %copy-done, bf16[1280,384]{1,0:T(8,128)(2,1)} %w_qkv.1, bf16[128,1280]{1,0:T(8,128)(2,1)} %w_out.1), custom_call_target="tpu_custom_call" | custom-call | tf_op jit(solution)/shard_map/attend/pallas_call | solution.py:429
  39.3 0.7 %copy.8 = bf16[1,64,1280]{2,1,0:T(8,128)(2,1)} copy(bf16[1,64,1280]{2,1,0:T(8,128)(2,1)S(1)} %attend.1) | data formatting | bytes 327680
Async XLA Ops:
  0.0 0.7 %copy-start.2 = (s32[1,32]{1,0:T(1,128)S(1)}, s32[1,32]{1,0:T(1,128)}, u32[]{:S(2)}) copy-start(s32[1,32]{1,0:T(1,128)} %plan.1) | copy-start | bytes 388
  0.0 0.7 %copy-start.1 = (s32[1,64,1]{1,2,0:T(1,128)S(1)}, s32[1,64,1]{1,2,0:T(1,128)}, u32[]{:S(2)}) copy-start(s32[1,64,1]{1,2,0:T(1,128)} %param.7) | copy-start | bytes 772
  0.7 0.7 %copy-start = (f32[1280]{0:T(1024)S(1)}, f32[1280]{0:T(1024)}, u32[]{:S(2)}) copy-start(f32[1280]{0:T(1024)} %gain.1) | copy-start | bytes 15364

commit v17 on v16

--- a/solution.py
+++ b/solution.py
@@ -36,7 +36,7 @@
 def kernel(
     frames, dest, plan, gain, w_qkv, w_out, out,
     raw, dest_v, plan_v, gain_v, xb, w, wo, sb, line_g, rb, gb, key_mark, query_mark, vd, co, cb, acc, top_v,
-    sum_v, near, sem, line_x, line_y, line_z,
+    sum_v, near, spare, spare_g, sem, line_x, line_y, line_z,
 ):
     g = lax.axis_index("grp")
     r = lax.axis_index("rep")
@@ -71,11 +71,23 @@
     def local(src, dst, s):
         return pltpu.make_async_copy(src, dst, sem.at[s])
 
-    def push(src, dst, ssem, rsem, tx, ty, tz, tc):
-        remote(src, dst, ssem, rsem, at(tx, ty, tz, tc)).start()
+    def push(src, dst, ssem, rsem, tx, ty, tz, tc, dummy):
+        if dummy is None:
+            remote(src, dst, ssem, rsem, at(tx, ty, tz, tc)).start()
+            return
+        same = (ty == y) & (tz == z) & (tc == c)
+
+        @pl.when(jnp.logical_not(same))
+        def _():
+            remote(src, dst, ssem, rsem, at(tx, ty, tz, tc)).start()
+
+        @pl.when(same)
+        def _():
+            local(src, dst, rsem).start()
+            local(src, dummy, ssem).start()
 
     def plane_of(i):
-        return lax.rem(2 * lax.rem(y + i, 4) + 1 + 5 * c, 8)
+        return lax.rem(y + i, 4) + 4 * (1 - c)
 
     def drain(ref, s):
         local(ref, ref, s).wait()
@@ -164,7 +176,7 @@
             for k in (2, 1, 3, 0):
                 push(
                     sb.at[i, 4 * s + turn_x(k)], rb.at[kind, cls, pl.ds(slot * HALF, HALF)],
-                    SBS, QR + kind, turn_x(k), ty, tz, cls,
+                    SBS, QR + kind, turn_x(k), ty, tz, cls, None if k else spare.at[0],
                 )
 
     loads[4].wait()
@@ -183,7 +195,8 @@
             group_copy(i).wait_recv()
         tz = plane_of(i)
         for k in (2, 1, 3, 0):
-            push(line_g.at[i], gb.at[cls, slot], GS, GR, turn_x(k), y, tz, cls)
+            push(line_g.at[i], gb.at[cls, slot], GS, GR, turn_x(k), y, tz, cls,
+                 None if k else spare_g)
     remote(w_qkv, w.at[1 - c], WS, WR, sibling).wait_recv()
     project(0, 1, 1 - c)
     opposite = lax.rem(y + 2, 4)
@@ -274,8 +287,7 @@
         vd[half, 0:512, :] = jnp.where(low, vals, turned)
         vd[half, 512:1024, :] = jnp.where(low, turned, vals)
 
-    owner_c = 1 - lax.rem(z, 2)
-    owner_y = lax.div(lax.rem(z + 2 * owner_c, 8), 2)
+    owner_y, owner_c = lax.rem(z, 4), 1 - lax.div(z, 4)
     away = lax.rem(y + 4 - owner_y, 4)
     place = away + lax.div(away, 2) * (5 - 2 * away)
     scale = 0.125 * math.log2(math.e)
@@ -326,7 +338,7 @@
             push(
                 co.at[pl.ds(128 * m + HALF * turn_x(k), HALF)],
                 cb.at[place, lax.div(x, 2), lax.rem(x, 2)],
-                CS, CR + lax.div(place, 3), turn_x(k), owner_y, 2 * m + c, owner_c,
+                CS, CR + lax.div(place, 3), turn_x(k), owner_y, 2 * m + c, owner_c, None if k else spare.at[1],
             )
 
     spread_values(c)
@@ -417,6 +429,8 @@
     pltpu.VMEM((4, 256, 1), F32),
     pltpu.VMEM((4, 256, 1), F32),
     pltpu.VMEM((ROWS, D), F32),
+    pltpu.VMEM((2, HALF, 128), BF),
+    pltpu.VMEM((1, 128), F32),
     pltpu.SemaphoreType.DMA((NSEM,)),
     pltpu.SemaphoreType.REGULAR,
     pltpu.SemaphoreType.REGULAR,

time: 40.1 us -> 39.9 us (level)
  the two profiles are of different devices: /device:TPU:1 before, /device:TPU:2 now
where the time goes in v17:
time: 39.9 us; the launch traced here: 39.7 us
  Pallas kernels  37.7 us (94%)
  local copies, waits for them, and re-layouts  2.03 us (5%)
    pallas_call x1, Pallas kernels, shards(): pl.pallas_call(kernel, out_shape=jax.ShapeDtypeStruct((1, ROWS, D), BF),...  37.7 us
    unnamed x7, local copies, waits for them, and re-layouts  2.03 us

profile of v17, /device:TPU:2, one launch (start us, length us, event | category | flops | bytes accessed | tf_op | source)
XLA Modules:
  0.0 39.7 jit_solution(16690069185393508353)
XLA Ops:
  0.0 0.0 copy-start.2
  0.0 0.0 copy-start.1
  0.0 0.7 %copy-done.2 = s32[1,32]{1,0:T(1,128)S(1)} copy-done((s32[1,32]{1,0:T(1,128)S(1)}, s32[1,32]{1,0:T(1,128)}, u32[]{:S(2)}) %copy-start.2) | copy-done | bytes 152
  0.7 0.0 copy-done.1
  0.7 0.0 copy-start
  0.7 0.7 %copy-done = f32[1280]{0:T(1024)S(1)} copy-done((f32[1280]{0:T(1024)S(1)}, f32[1280]{0:T(1024)}, u32[]{:S(2)}) %copy-start) | copy-done | bytes 5144
  1.4 37.7 %attend.1 = bf16[1,64,1280]{2,1,0:T(8,128)(2,1)S(1)} custom-call(bf16[1,64,1280]{2,1,0:T(8,128)(2,1)} %frames.1, s32[1,64]{1,0:T(1,128)S(1)} %bitcast.1, s32[1,32]{1,0:T(1,128)S(1)} %copy-done.2, f32[1280]{0:T(1024)S(1)} %copy-done, bf16[1280,384]{1,0:T(8,128)(2,1)} %w_qkv.1, bf16[128,1280]{1,0:T(8,128)(2,1)} %w_out.1), custom_call_target="tpu_custom_call" | custom-call | tf_op jit(solution)/shard_map/attend/pallas_call | solution.py:443
  39.1 0.7 %copy.8 = bf16[1,64,1280]{2,1,0:T(8,128)(2,1)} copy(bf16[1,64,1280]{2,1,0:T(8,128)(2,1)S(1)} %attend.1) | data formatting | bytes 327680
Async XLA Ops:
  0.0 0.7 %copy-start.2 = (s32[1,32]{1,0:T(1,128)S(1)}, s32[1,32]{1,0:T(1,128)}, u32[]{:S(2)}) copy-start(s32[1,32]{1,0:T(1,128)} %plan.1) | copy-start | bytes 388
  0.0 0.7 %copy-start.1 = (s32[1,64,1]{1,2,0:T(1,128)S(1)}, s32[1,64,1]{1,2,0:T(1,128)}, u32[]{:S(2)}) copy-start(s32[1,64,1]{1,2,0:T(1,128)} %param.7) | copy-start | bytes 772
  0.7 0.7 %copy-start = (f32[1280]{0:T(1024)S(1)}, f32[1280]{0:T(1024)}, u32[]{:S(2)}) copy-start(f32[1280]{0:T(1024)} %gain.1) | copy-start | bytes 15364

commit v18 on v17

--- a/solution.py
+++ b/solution.py
@@ -87,7 +87,7 @@
             local(src, dummy, ssem).start()
 
     def plane_of(i):
-        return lax.rem(y + i, 4) + 4 * (1 - c)
+        return lax.rem(y + i + 1 - c, 4) + 4 * (1 - c)
 
     def drain(ref, s):
         local(ref, ref, s).wait()
@@ -287,7 +287,7 @@
         vd[half, 0:512, :] = jnp.where(low, vals, turned)
         vd[half, 512:1024, :] = jnp.where(low, turned, vals)
 
-    owner_y, owner_c = lax.rem(z, 4), 1 - lax.div(z, 4)
+    owner_y, owner_c = lax.rem(z + 3 * lax.div(z, 4), 4), 1 - lax.div(z, 4)
     away = lax.rem(y + 4 - owner_y, 4)
     place = away + lax.div(away, 2) * (5 - 2 * away)
     scale = 0.125 * math.log2(math.e)

time: 39.9 us -> 39.6 us (level)
  the two profiles are of different devices: /device:TPU:2 before, /device:TPU:64 now
where the time goes in v18:
time: 39.6 us; the launch traced here: 39.5 us
  Pallas kernels  37.4 us (94%)
  local copies, waits for them, and re-layouts  2.03 us (5%)
    pallas_call x1, Pallas kernels, shards(): pl.pallas_call(kernel, out_shape=jax.ShapeDtypeStruct((1, ROWS, D), BF),...  37.4 us
    unnamed x7, local copies, waits for them, and re-layouts  2.03 us

profile of v18, /device:TPU:64, one launch (start us, length us, event | category | flops | bytes accessed | tf_op | source)
XLA Modules:
  0.0 39.5 jit_solution(7306064145206570974)
XLA Ops:
  0.0 0.0 copy-start.2
  0.0 0.0 copy-start.1
  0.0 0.7 %copy-done.2 = s32[1,32]{1,0:T(1,128)S(1)} copy-done((s32[1,32]{1,0:T(1,128)S(1)}, s32[1,32]{1,0:T(1,128)}, u32[]{:S(2)}) %copy-start.2) | copy-done | bytes 152
  0.7 0.0 copy-done.1
  0.7 0.0 copy-start
  0.7 0.7 %copy-done = f32[1280]{0:T(1024)S(1)} copy-done((f32[1280]{0:T(1024)S(1)}, f32[1280]{0:T(1024)}, u32[]{:S(2)}) %copy-start) | copy-done | bytes 5144
  1.4 37.4 %attend.1 = bf16[1,64,1280]{2,1,0:T(8,128)(2,1)S(1)} custom-call(bf16[1,64,1280]{2,1,0:T(8,128)(2,1)} %frames.1, s32[1,64]{1,0:T(1,128)S(1)} %bitcast.1, s32[1,32]{1,0:T(1,128)S(1)} %copy-done.2, f32[1280]{0:T(1024)S(1)} %copy-done, bf16[1280,384]{1,0:T(8,128)(2,1)} %w_qkv.1, bf16[128,1280]{1,0:T(8,128)(2,1)} %w_out.1), custom_call_target="tpu_custom_call" | custom-call | tf_op jit(solution)/shard_map/attend/pallas_call | solution.py:443
  38.8 0.7 %copy.8 = bf16[1,64,1280]{2,1,0:T(8,128)(2,1)} copy(bf16[1,64,1280]{2,1,0:T(8,128)(2,1)S(1)} %attend.1) | data formatting | bytes 327680
Async XLA Ops:
  0.0 0.7 %copy-start.2 = (s32[1,32]{1,0:T(1,128)S(1)}, s32[1,32]{1,0:T(1,128)}, u32[]{:S(2)}) copy-start(s32[1,32]{1,0:T(1,128)} %plan.1) | copy-start | bytes 388
  0.0 0.7 %copy-start.1 = (s32[1,64,1]{1,2,0:T(1,128)S(1)}, s32[1,64,1]{1,2,0:T(1,128)}, u32[]{:S(2)}) copy-start(s32[1,64,1]{1,2,0:T(1,128)} %param.7) | copy-start | bytes 772
  0.7 0.7 %copy-start = (f32[1280]{0:T(1024)S(1)}, f32[1280]{0:T(1024)}, u32[]{:S(2)}) copy-start(f32[1280]{0:T(1024)} %gain.1) | copy-start | bytes 15364
